TPU v7x, 256 devices: a whole 4x4x8 slice. The times are simulated.
256 devices in a mesh: step: 16 (over x, y), seq: 16 (over z, core).
Axes of the slice: x: 4, y: 4, z: 8, core: 2. Of those that a mesh axis runs over, the one named last changes fastest.
Arguments:
- states: float32 [16, 4096, 1280], P('step', 'seq'), may hold values from -6 to 6
- start: float32 [4096, 1280], P('seq'), may hold values from -6 to 6
- noise: bfloat16 [16, 4096, 1280], P('step', 'seq'), may hold values from -6 to 6
- coefficients: float32 [16, 3], P('step'), may hold values from 0.05 to 0.4
- context: bfloat16 [16, 4096, 1024], P('step', None, 'seq'), may hold values from -6 to 6
- qkv_weight: bfloat16 [1280, 3072], P('step'), may hold values from -5 to 5, as said below
- out_weights: bfloat16 [2, 1024, 1280], P(None, 'step'), may hold values from -0.1875 to 0.1875
- gain: float32 [1280], replicated, may hold values from 0.5 to 1.5
Outputs:
- advanced: float32 [16, 4096, 1280], P('step', 'seq')
- mixed: float32 [16, 4096, 1280], P('step', 'seq')
Inputs may be any that keep to these rules, and one draw needn't show every extreme that they name: `qkv_weight`: entries within 40 / sqrt(1280) in magnitude.
All inputs are finite; a program needn't handle non-finite values.
Results may differ from a plain program's by a relative error of at most 0.002.
Values may be sent and summed in bfloat16 or wider, within the bound.
No kernel may reach another device: no remote copies, remote signals or barrier semaphores. Data moves between devices by JAX's collectives and lax.ppermute only.
A program may use at most 128 MiB of HBM per device.

v0:
```python
import jax
import jax.numpy as jnp
from jax import lax
from jax.experimental import pallas as pl
from jax.experimental.pallas import tpu as pltpu
from jax.sharding import PartitionSpec as P

HEAD_DIM = 64
GRANT = 60 * 2**20


def attention_kernel(qkv_ref, out_ref, value_rows, scores, tops):
    turn, turns = pl.program_id(0), pl.num_programs(0)
    blocks, _, dim, rows = qkv_ref.shape
    taken = out_ref.shape[0]

    @pl.when(turn == 0)
    def _():
        for j in range(blocks):
            values = qkv_ref[j, 2].astype(jnp.float32)
            padded = jnp.concatenate([values, jnp.ones((dim, rows), jnp.float32)], axis=0)
            value_rows[j * rows : (j + 1) * rows, :] = padded.T.astype(jnp.bfloat16)

    def score(which, slot):
        queries = []
        for b in range(taken):
            query = qkv_ref[which * taken + b, 0].astype(jnp.float32) * (HEAD_DIM**-0.5)
            query = jnp.concatenate([query, query], axis=0).T[:, :dim]
            queries.append(query.astype(jnp.bfloat16))
        queries = jnp.concatenate(queries, axis=0)
        top = None
        for j in range(blocks):
            part = jnp.dot(queries, qkv_ref[j, 1], preferred_element_type=jnp.float32)
            scores[slot, :, j * rows : (j + 1) * rows] = part
            for first in range(0, rows, 128):
                piece = part[:, first : first + 128]
                top = piece if top is None else jnp.maximum(top, piece)
        tops[slot] = jnp.broadcast_to(jnp.max(top, axis=-1, keepdims=True), top.shape)

    def finish(slot):
        top = tops[slot][:, :1]
        total = jnp.zeros((taken * rows, 2 * dim), jnp.float32)
        for j in range(blocks):
            keys = slice(j * rows, (j + 1) * rows)
            weights = jnp.exp(scores[slot, :, keys] - top).astype(jnp.bfloat16)
            total = total + jnp.dot(weights, value_rows[keys, :], preferred_element_type=jnp.float32)
        total = total.T
        attended = (total[:dim] / total[dim:]).astype(jnp.bfloat16)
        for b in range(taken):
            out_ref[b] = attended[:, b * rows : (b + 1) * rows]

    @pl.when(turn == 0)
    def _():
        score(0, 0)

    for slot in (0, 1):

        @pl.when((lax.rem(turn, 2) == slot) & (turn < turns - 1))
        def _():
            score(turn + 1, 1 - slot)
            finish(slot)

        @pl.when((lax.rem(turn, 2) == slot) & (turn == turns - 1))
        def _():
            finish(slot)


def attend(qkv):
    blocks, _, dim, rows = qkv.shape
    taken = 4
    return pl.pallas_call(
        attention_kernel,
        out_shape=jax.ShapeDtypeStruct((blocks, dim, rows), jnp.bfloat16),
        grid=(blocks // taken,),
        in_specs=[pl.BlockSpec(qkv.shape, lambda i: (0, 0, 0, 0))],
        out_specs=pl.BlockSpec((taken, dim, rows), lambda i: (i, 0, 0)),
        scratch_shapes=[
            pltpu.VMEM((blocks * rows, 2 * dim), jnp.bfloat16),
            pltpu.VMEM((2, taken * rows, blocks * rows), jnp.float32),
            pltpu.VMEM((2, taken * rows, 128), jnp.float32),
        ],
        compiler_params=pltpu.CompilerParams(
            dimension_semantics=("arbitrary",), vmem_limit_bytes=48 * 2**20
        ),
        cost_estimate=pl.CostEstimate(
            flops=16 * 2**30, bytes_accessed=3 * 2**20, transcendentals=2**24
        ),
    )(qkv)


def position(seq_ref):
    return lax.rem(seq_ref[0], 2), lax.div(seq_ref[0], 2)


def tiles(count):
    for n in range(3 * count):
        yield slice(16 * (n // 3), 16 * (n // 3) + 16), 128 * (n % 3), 16 * (n // 5), 128 * (n % 5)


def cut_kernel(seq_ref, context_ref, qkv_ref, weights_ref, first_ref, last_ref, *refs):
    *pieces, context, shard, last, done, sent = refs
    core, chip = position(seq_ref)
    chips = len(pieces) + 1
    depth, half, width = weights_ref.shape[1], first_ref.shape[2], pieces[0].shape[1]
    inner = qkv_ref.shape[1] // 3
    shard[depth:, :] = jnp.zeros((shard.shape[0] - depth, half), jnp.bfloat16)
    loads = [
        pltpu.make_async_copy(
            weights_ref.at[0, :, pl.ds(pl.multiple_of(core * half, half), half)],
            shard.at[:depth],
            done.at[0],
        )
    ]
    for n, (rows, column, low, left) in enumerate(tiles(3)):
        first_row = pl.multiple_of(32 * core + rows.start, 16)
        first_column = pl.multiple_of(column // 128 * inner + 128 * chip, 128)
        loads.append(
            pltpu.make_async_copy(
                qkv_ref.at[pl.ds(first_row, 16), pl.ds(first_column, 128)],
                shard.at[depth + low : depth + low + 16, left : left + 128],
                done.at[3 + n],
            )
        )
    load_context = pltpu.make_async_copy(context_ref, context, done.at[1])
    load_last = pltpu.make_async_copy(weights_ref.at[1], last, done.at[2])
    for load in (*loads, load_context, load_last):
        load.start()
    for load in loads:
        load.wait()
    stores = []
    for i in range(first_ref.shape[0]):
        stores.append(pltpu.make_async_copy(shard, first_ref.at[i], sent.at[chips + i]))
        stores[-1].start()
    load_context.wait()
    for k, piece in enumerate(pieces):
        target = lax.rem(chip + k + 1, chips)
        tokens = pl.ds(pl.multiple_of(target * width, width), width)
        stores.append(pltpu.make_async_copy(context.at[:, tokens], piece, sent.at[k]))
        stores[-1].start()
    load_last.wait()
    stores.append(pltpu.make_async_copy(last, last_ref, sent.at[chips - 1]))
    stores[-1].start()
    for store in stores:
        store.wait()


def cut(seq, context, qkv_weight, out_weights, steps, chips):
    dim, tokens = context.shape
    _, depth, width = out_weights.shape
    far = pl.BlockSpec(memory_space=pl.ANY)
    shapes = [(steps, depth + 32, width // 2), (depth, width)] + [(dim, tokens // chips)] * (chips - 1)
    return pl.pallas_call(
        cut_kernel,
        out_shape=[jax.ShapeDtypeStruct(shape, jnp.bfloat16) for shape in shapes],
        in_specs=[pl.BlockSpec(memory_space=pltpu.SMEM)] + [far] * 3,
        out_specs=[far] * len(shapes),
        scratch_shapes=[
            pltpu.VMEM(context.shape, jnp.bfloat16),
            pltpu.VMEM(shapes[0][1:], jnp.bfloat16),
            pltpu.VMEM(shapes[1], jnp.bfloat16),
            pltpu.SemaphoreType.DMA((12,)),
            pltpu.SemaphoreType.DMA((chips + steps,)),
        ],
        compiler_params=pltpu.CompilerParams(vmem_limit_bytes=GRANT),
        cost_estimate=pl.CostEstimate(flops=0, bytes_accessed=4 * 2**20, transcendentals=0),
    )(seq, context, qkv_weight, out_weights)


def collect_kernel(seq_ref, context_ref, *refs):
    *pieces, packed_ref, kept_ref, given_ref, slices_ref, _, arrived, slices, done, sent = refs
    core, chip = position(seq_ref)
    chips = len(pieces) + 1
    rows = kept_ref.shape[2]
    depth = packed_ref.shape[1] - 32
    own = context_ref.at[:, pl.ds(pl.multiple_of(2 * rows * chip, 2 * rows), 2 * rows)]
    loads = []
    for k, piece in enumerate((own, *pieces)):
        source = lax.rem(chip - k + chips, chips)
        loads.append(pltpu.make_async_copy(piece, arrived.at[source], done.at[9 + k]))
        loads[-1].start()
    unpacks = []
    for n, (place, column, low, left) in enumerate(tiles(3)):
        unpacks.append(
            pltpu.make_async_copy(
                packed_ref.at[:, depth + low : depth + low + 16, left : left + 128],
                slices.at[:, place, column : column + 128],
                done.at[n],
            )
        )
        unpacks[-1].start()
    for load in loads:
        load.wait()
    stores = []
    for turn, (side, out_ref) in enumerate(((1 - core, given_ref), (core, kept_ref))):
        tokens = pl.ds(pl.multiple_of(side * rows, rows), rows)
        stores.append(pltpu.make_async_copy(arrived.at[:, :, tokens], out_ref, sent.at[turn]))
        stores[-1].start()
    for unpack in unpacks:
        unpack.wait()
    stores.append(pltpu.make_async_copy(slices, slices_ref, sent.at[2]))
    stores[-1].start()
    for store in stores:
        store.wait()


def collect(seq, context, pieces, packed):
    dim, width = pieces[0].shape
    chips = len(pieces) + 1
    shape = (packed.shape[0], 48, 384)
    far = pl.BlockSpec(memory_space=pl.ANY)
    return pl.pallas_call(
        collect_kernel,
        out_shape=(jax.ShapeDtypeStruct((chips, dim, width // 2), jnp.bfloat16),) * 2
        + (
            jax.ShapeDtypeStruct(shape, jnp.bfloat16),
            jax.ShapeDtypeStruct(packed.shape, jnp.bfloat16),
        ),
        in_specs=[pl.BlockSpec(memory_space=pltpu.SMEM)] + [far] * (chips + 1),
        out_specs=(far,) * 4,
        input_output_aliases={chips + 1: 3},
        scratch_shapes=[
            pltpu.VMEM((chips, dim, width), jnp.bfloat16),
            pltpu.VMEM(shape, jnp.bfloat16),
            pltpu.SemaphoreType.DMA((9 + chips,)),
            pltpu.SemaphoreType.DMA((3,)),
        ],
        compiler_params=pltpu.CompilerParams(vmem_limit_bytes=GRANT),
        cost_estimate=pl.CostEstimate(flops=0, bytes_accessed=2**20, transcendentals=0),
    )(seq, context, *pieces, packed)


def drift_kernel(
    seq_ref, factors_ref, kept_ref, taken_ref, mine_ref, other_ref, states_ref, noise_ref,
    drift_ref, context, weights, states, noise, drift, done,
):
    core, _ = position(seq_ref)
    chips, _, dim, rows = context.shape
    half = weights.shape[3]
    loads = [
        pltpu.make_async_copy(kept_ref, context.at[:, core], done.at[0]),
        pltpu.make_async_copy(taken_ref, context.at[:, 1 - core], done.at[1]),
        pltpu.make_async_copy(mine_ref.at[:, :dim, :], weights.at[0], done.at[2]),
        pltpu.make_async_copy(other_ref.at[:, :dim, :], weights.at[1], done.at[3]),
        pltpu.make_async_copy(states_ref, states, done.at[4]),
        pltpu.make_async_copy(noise_ref, noise, done.at[5]),
    ]
    for load in loads:
        load.start()
    loads[0].wait()
    loads[1].wait()
    token_rows = context[...].reshape(chips * 2 * dim, rows).T
    stores = []
    for turn, side in enumerate((core, 1 - core)):
        loads[2 + turn].wait()
        weight = weights[turn].reshape(chips * 2 * dim, half)
        product = jnp.dot(token_rows, weight, preferred_element_type=jnp.float32)
        if turn == 0:
            loads[4].wait()
            loads[5].wait()
        columns = pl.ds(pl.multiple_of(side * half, half), half)
        drift[:, columns] = (
            (factors_ref[0] + factors_ref[1]) * states[:, columns]
            + factors_ref[1] * product
            + factors_ref[2] * noise[:, columns].astype(jnp.float32)
        )
        stores.append(
            pltpu.make_async_copy(drift.at[:, columns], drift_ref.at[:, columns], done.at[6 + turn])
        )
        stores[-1].start()
    for store in stores:
        store.wait()


def drift_of(seq, factors, kept, taken, mine, other, states, noise):
    chips, dim, rows = kept.shape
    scalars = pl.BlockSpec(memory_space=pltpu.SMEM)
    far = pl.BlockSpec(memory_space=pl.ANY)
    return pl.pallas_call(
        drift_kernel,
        out_shape=jax.ShapeDtypeStruct(states.shape, jnp.float32),
        in_specs=[scalars] * 2 + [far] * 6,
        out_specs=far,
        scratch_shapes=[
            pltpu.VMEM((chips, 2, dim, rows), jnp.bfloat16),
            pltpu.VMEM((2, mine.shape[0], dim, mine.shape[2]), jnp.bfloat16),
            pltpu.VMEM(states.shape, jnp.float32),
            pltpu.VMEM(states.shape, jnp.bfloat16),
            pltpu.VMEM(states.shape, jnp.float32),
            pltpu.SemaphoreType.DMA((8,)),
        ],
        compiler_params=pltpu.CompilerParams(vmem_limit_bytes=GRANT),
        cost_estimate=pl.CostEstimate(
            flops=2**11 * states.size, bytes_accessed=8 * 2**20, transcendentals=0
        ),
    )(seq, factors, kept, taken, mine, other, states, noise)


def sum_kernel(drifts_ref, start_ref, advanced_ref):
    running = start_ref[...]
    for j in range(drifts_ref.shape[0]):
        advanced_ref[j] = running
        running = running + drifts_ref[j]


def sum_before(drifts, start):
    whole = pl.BlockSpec(memory_space=pltpu.VMEM)
    return pl.pallas_call(
        sum_kernel,
        out_shape=jax.ShapeDtypeStruct(drifts.shape, jnp.float32),
        in_specs=[whole] * 2,
        out_specs=whole,
        compiler_params=pltpu.CompilerParams(vmem_limit_bytes=16 * 2**20),
        cost_estimate=pl.CostEstimate(
            flops=drifts.size, bytes_accessed=8 * drifts.size, transcendentals=0
        ),
    )(drifts, start)


def qkv_kernel(
    advanced_ref, gain_ref, slices_ref, out_ref, advanced, normed, weights, projected, done, sent
):
    _, _, dim, rows = out_ref.shape
    chips = slices_ref.shape[0] // 2
    steps, depth, _ = weights.shape
    columns, upper = slices_ref.shape[3], slices_ref.shape[2]
    load_rows = pltpu.make_async_copy(advanced_ref, advanced, done.at[2 * chips])
    load_rows.start()
    loads = []
    for c in range(chips):
        place = slice(c * columns, (c + 1) * columns)
        rest = depth - upper
        loads.append(
            (
                pltpu.make_async_copy(
                    slices_ref.at[2 * c], weights.at[:, :upper, place], done.at[2 * c]
                ),
                pltpu.make_async_copy(
                    slices_ref.at[2 * c + 1, :, upper - rest :],
                    weights.at[:, upper:, place],
                    done.at[2 * c + 1],
                ),
            )
        )
    for pair in loads[:4]:
        for load in pair:
            load.start()
    load_rows.wait()
    gain = gain_ref[...]
    part_rows = 32
    for first in range(0, rows, part_rows):
        some = advanced[first : first + part_rows, :]
        mean = jnp.mean(some, axis=-1, keepdims=True)
        centred = some - mean
        variance = jnp.mean(centred * centred, axis=-1, keepdims=True)
        normed[first : first + part_rows, :] = (
            centred * lax.rsqrt(variance + 1e-05) * gain
        ).astype(jnp.bfloat16)
    stores = []
    for c in range(0, chips, 2):
        for pair in loads[c : c + 2]:
            for load in pair:
                load.wait()
        for pair in loads[c + 4 : c + 6]:
            for load in pair:
                load.start()
        weight = weights[:, :, c * columns : (c + 2) * columns].reshape(steps * depth, 2 * columns)
        part = jnp.dot(normed[...], weight, preferred_element_type=jnp.float32)
        part = part.T.astype(jnp.bfloat16).reshape(2, 3, 2, dim, rows)
        for b in (0, 1):
            for kind in range(3):
                projected[2 * (c + b) : 2 * (c + b) + 2, kind] = part[b, kind]
        heads = slice(2 * c, 2 * c + 4)
        stores.append(
            pltpu.make_async_copy(projected.at[heads], out_ref.at[heads], sent.at[c // 2])
        )
        stores[-1].start()
    for store in stores:
        store.wait()


def project_qkv(advanced, gain, slices, depth, dim):
    rows, width = advanced.shape
    heads, steps, _, columns = slices.shape
    shape = (heads, 3, dim, rows)
    far = pl.BlockSpec(memory_space=pl.ANY)
    return pl.pallas_call(
        qkv_kernel,
        out_shape=jax.ShapeDtypeStruct(shape, jnp.bfloat16),
        in_specs=[far, pl.BlockSpec(memory_space=pltpu.VMEM), far],
        out_specs=far,
        scratch_shapes=[
            pltpu.VMEM(advanced.shape, jnp.float32),
            pltpu.VMEM(advanced.shape, jnp.bfloat16),
            pltpu.VMEM((steps, depth, columns * heads // 2), jnp.bfloat16),
            pltpu.VMEM(shape, jnp.bfloat16),
            pltpu.SemaphoreType.DMA((heads + 1,)),
            pltpu.SemaphoreType.DMA((heads // 4,)),
        ],
        compiler_params=pltpu.CompilerParams(vmem_limit_bytes=GRANT),
        cost_estimate=pl.CostEstimate(
            flops=6 * rows * width * heads * dim, bytes_accessed=10 * 2**20, transcendentals=0
        ),
    )(advanced, gain.reshape(1, -1), slices)


def mix_kernel(
    attended_ref, weight_ref, advanced_ref, copied_ref, mixed_ref,
    weight, advanced, mixed, done, sent,
):
    rows, width = advanced.shape
    chunks = weight.shape[0]
    wide = width // chunks
    load_advanced = pltpu.make_async_copy(advanced_ref, advanced, done.at[chunks + 1])
    loads = [
        pltpu.make_async_copy(weight_ref.at[:, b * wide : (b + 1) * wide], weight.at[b], done.at[b])
        for b in range(chunks)
    ]
    for load in (*loads, load_advanced):
        load.start()
    token_rows = attended_ref[...].T
    stores = []
    for b in range(chunks):
        columns = slice(b * wide, (b + 1) * wide)
        loads[b].wait()
        product = jnp.dot(token_rows, weight[b], preferred_element_type=jnp.float32)
        if b == 0:
            load_advanced.wait()
            stores.append(pltpu.make_async_copy(advanced, copied_ref, sent.at[chunks]))
            stores[-1].start()
        mixed[:, columns] = advanced[:, columns] + product
        stores.append(
            pltpu.make_async_copy(mixed.at[:, columns], mixed_ref.at[:, columns], sent.at[b])
        )
        stores[-1].start()
    for store in stores:
        store.wait()


def mix(attended, weight, advanced):
    depth, rows = attended.shape
    width = advanced.shape[1]
    chunks = width // 256
    far = pl.BlockSpec(memory_space=pl.ANY)
    return pl.pallas_call(
        mix_kernel,
        out_shape=(jax.ShapeDtypeStruct(advanced.shape, jnp.float32),) * 2,
        in_specs=[pl.BlockSpec(memory_space=pltpu.VMEM), far, far],
        out_specs=(far, far),
        scratch_shapes=[
            pltpu.VMEM((chunks, depth, width // chunks), jnp.bfloat16),
            pltpu.VMEM(advanced.shape, jnp.float32),
            pltpu.VMEM(advanced.shape, jnp.float32),
            pltpu.SemaphoreType.DMA((chunks + 2,)),
            pltpu.SemaphoreType.DMA((chunks + 1,)),
        ],
        compiler_params=pltpu.CompilerParams(vmem_limit_bytes=56 * 2**20),
        cost_estimate=pl.CostEstimate(
            flops=2 * rows * depth * width, bytes_accessed=8 * 2**20, transcendentals=0
        ),
    )(attended, weight, advanced)


def swap(blocks, axis):
    return lax.all_to_all(blocks, axis, split_axis=0, concat_axis=0, tiled=True)


def local(states, start, noise, coefficients, context, qkv_weight, out_weights, gain):
    steps, seqs = lax.axis_size("step"), lax.axis_size("seq")
    step, seq = lax.axis_index("step"), lax.axis_index("seq")
    rows, width = start.shape
    tokens, dim = context.shape[1:]

    heads, chips = seqs, seqs // 2
    place = seq.astype(jnp.int32).reshape(1)
    pairs = [(i, i ^ 1) for i in range(seqs)]
    heads_tokens = context[0].T

    first_half, last_shard, *pieces = cut(
        place, heads_tokens, qkv_weight, out_weights, steps, chips
    )
    packed = swap(first_half, "step")

    pieces = [
        lax.ppermute(piece, "seq", [(i, (i + 2 * k + 2) % seqs) for i in range(seqs)])
        for k, piece in enumerate(pieces)
    ]
    kept, given, slices, mine = collect(place, heads_tokens, pieces, packed)
    slices = lax.all_gather(slices, "seq")
    taken = lax.ppermute(given, "seq", pairs)
    other = lax.ppermute(mine, "seq", pairs)
    drift = drift_of(place, coefficients[0], kept, taken, mine, other, states[0], noise[0])

    piece = rows // steps
    drifts = swap(drift.reshape(steps, piece, width), "step")
    advanced = sum_before(drifts, lax.dynamic_slice_in_dim(start, step * piece, piece, 0))
    advanced = swap(advanced, "step").reshape(rows, width)
    by_head = swap(project_qkv(advanced, gain, slices, qkv_weight.shape[0], dim), "seq")
    last_weight = lax.all_gather(last_shard, "step", axis=0, tiled=True)
    attended = swap(attend(by_head), "seq").reshape(seqs * dim, rows)
    advanced, mixed = mix(attended, last_weight, advanced)
    return (advanced[None], mixed[None])


def solution(mesh):
    placed = (
        P("step", "seq", None),
        P("seq", None),
        P("step", "seq", None),
        P("step", None),
        P("step", None, "seq"),
        P("step", None),
        P(None, "step", None),
        P(),
    )
    return jax.shard_map(
        local,
        mesh=mesh,
        in_specs=placed,
        out_specs=(P("step", "seq", None), P("step", "seq", None)),
        check_vma=False,
    )
```

profile of v0, /device:TPU:1, one launch (start us, length us, event | category | flops | bytes accessed | tf_op | source)
XLA Modules:
  0.0 222.9 jit_solution(11581362511904025176)
XLA Ops:
  8.0 2.8 %shard_map.95 = (bf16[16,96,640]{2,1,0:T(8,128)(2,1)}, bf16[64,1280]{1,0:T(8,128)(2,1)}, bf16[64,512]{1,0:T(8,128)(2,1)}, bf16[64,512]{1,0:T(8,128)(2,1)}, bf16[...) custom-call(s32[1]{0:T(128)} %bitcast.seq_ref, ...), custom_call_target="tpu_custom_call" | custom-call | bytes 4194304 | tf_op jit(solution)/shard_map/pallas_call | solution.py:152
  10.8 7.6 %all-to-all-start = ((bf16[16,96,640]{2,1,0:T(8,128)(2,1)}), bf16[16,96,640]{2,1,0:T(8,128)(2,1)S(1)}, u32[]{:S(2)}, u32[]{:S(2)}) async-start(bf16[16,96,640]{2,1,0:T(8,128)(2,1)} %get-tuple-element.24), calls=%async_computation | async-start | bytes 3932160 | tf_op jit(solution)/shard_map/all_to_all | solution.py:464
  18.4 1.7 collective-permute-start
  20.2 3.0 %collective-permute-start.1 = (bf16[64,512]{1,0:T(8,128)(2,1)}, bf16[64,512]{1,0:T(8,128)(2,1)S(1)}, u32[]{:S(2)}, u32[]{:S(2)}) collective-permute-start(bf16[64,512]{1,0:T(8,128)(2,1)} %get-tuple-element.18), channel_id=1, source_target_pairs={{0,4},{1,5},{2,6},{3,7},{4,8},{5,9},{6,10},{7,11},{8,12},{9,13},{1... | collective-permute-start | bytes 196616 | tf_op jit(solution)/shard_map/ppermute | solution.py:484
  23.2 3.8 %collective-permute-start.2 = (bf16[64,512]{1,0:T(8,128)(2,1)}, bf16[64,512]{1,0:T(8,128)(2,1)S(1)}, u32[]{:S(2)}, u32[]{:S(2)}) collective-permute-start(bf16[64,512]{1,0:T(8,128)(2,1)} %get-tuple-element.19), channel_id=1, source_target_pairs={{0,6},{1,7},{2,8},{3,9},{4,10},{5,11},{6,12},{7,13},{8,14},{9,15},... | collective-permute-start | bytes 196616 | tf_op jit(solution)/shard_map/ppermute | solution.py:484
  27.4 4.5 %collective-permute-start.4 = (bf16[64,512]{1,0:T(8,128)(2,1)}, bf16[64,512]{1,0:T(8,128)(2,1)S(1)}, u32[]{:S(2)}, u32[]{:S(2)}) collective-permute-start(bf16[64,512]{1,0:T(8,128)(2,1)} %get-tuple-element.21), channel_id=1, source_target_pairs={{0,10},{1,11},{2,12},{3,13},{4,14},{5,15},{6,0},{7,1},{8,2},{9,3},... | collective-permute-start | bytes 196616 | tf_op jit(solution)/shard_map/ppermute | solution.py:484
  31.8 2.4 %collective-permute-start.5 = (bf16[64,512]{1,0:T(8,128)(2,1)}, bf16[64,512]{1,0:T(8,128)(2,1)S(1)}, u32[]{:S(2)}, u32[]{:S(2)}) collective-permute-start(bf16[64,512]{1,0:T(8,128)(2,1)} %get-tuple-element.22), channel_id=1, source_target_pairs={{0,12},{1,13},{2,14},{3,15},{4,0},{5,1},{6,2},{7,3},{8,4},{9,5},{1... | collective-permute-start | bytes 196616 | tf_op jit(solution)/shard_map/ppermute | solution.py:484
  35.0 7.2 %collective-permute-done.5.refs_5_ = bf16[64,512]{1,0:T(8,128)(2,1)S(1)} collective-permute-done((bf16[64,512]{1,0:T(8,128)(2,1)}, bf16[64,512]{1,0:T(8,128)(2,1)S(1)}, u32[]{:S(2)}, u32[]{:S(2)}) %collective-permute-start.5) | collective-permute-done | bytes 65568 | tf_op jit(solution)/shard_map/ppermute | solution.py:484
  45.6 2.3 %shard_map.96 = (bf16[8,64,256]{2,1,0:T(8,128)(2,1)}, bf16[8,64,256]{2,1,0:T(8,128)(2,1)}, bf16[16,48,384]{2,1,0:T(8,128)(2,1)}, bf16[16,96,640]{2,1,0:T(8,128)(2,1)}) custom-call(s32[1]{0:T(128)} %bitcast.seq_ref, bf16[64,4096]{1,0:T(8,128)(2,1)} %bitcast.18, bf16[64,512]{1,0:T(8,128)(2,1)} %copy-done.7, ...), custom_call_target="tpu_custom_call", output_to_operand_aliasing={{3}: (9, {})} | custom-call | bytes 1048576 | tf_op jit(solution)/shard_map/pallas_call | solution.py:211
  47.9 3.9 %collective-permute-start.8 = (bf16[16,96,640]{2,1,0:T(8,128)(2,1)}, bf16[16,96,640]{2,1,0:T(8,128)(2,1)S(1)}, u32[]{:S(2)}, u32[]{:S(2)}) collective-permute-start(bf16[16,96,640]{2,1,0:T(8,128)(2,1)} %get-tuple-element.27.mine_ref), channel_id=1, source_target_pairs={{0,1},{1,0},{2,3},{3,2},{4,5},{5,4},{6,7},{7,6},{8,9},{9,8},{10,11... | collective-permute-start | bytes 5898248 | tf_op jit(solution)/shard_map/ppermute | solution.py:490
  51.8 4.1 %collective-permute-done.7.taken_ref = bf16[8,64,256]{2,1,0:T(8,128)(2,1)S(1)} collective-permute-done((bf16[8,64,256]{2,1,0:T(8,128)(2,1)}, bf16[8,64,256]{2,1,0:T(8,128)(2,1)S(1)}, u32[]{:S(2)}, u32[]{:S(2)}) %collective-permute-start.7) | collective-permute-done | bytes 262176 | tf_op jit(solution)/shard_map/ppermute | solution.py:489
  57.4 4.8 %shard_map.97 = f32[256,1280]{1,0:T(8,128)} custom-call(s32[1]{0:T(128)} %bitcast.seq_ref, f32[3]{0:T(128)} %bitcast.22, bf16[8,64,256]{2,1,0:T(8,128)(2,1)} %get-tuple-element.25.kept_ref, bf16[8,64,256]{2,1,0:T(8,128)(2,1)} %copy-done.6, bf16[16,96,640]{2,1,0:T(8,128)(2,1)} %get-tuple-element.27.mine_ref, bf16[16,96,640]{2,1,0:T(8,128)(2,1)} %copy-done.5, ...), custom_call_target="tpu_custom_call" | custom-call | flops 671088640 | bytes 8388608 | tf_op jit(solution)/shard_map/pallas_call | solution.py:278
  62.2 3.7 %all-to-all-start.1 = ((f32[16,16,1280]{2,1,0:T(8,128)}), f32[16,16,1280]{2,1,0:T(8,128)S(1)}, u32[]{:S(2)}, u32[]{:S(2)}) async-start(f32[16,16,1280]{2,1,0:T(8,128)} %bitcast.16), calls=%async_computation.1 | async-start | bytes 2621440 | tf_op jit(solution)/shard_map/all_to_all | solution.py:464
  65.9 20.0 %all-to-all-done.1.drifts_ref = f32[16,16,1280]{2,1,0:T(8,128)S(1)} async-done(((f32[16,16,1280]{2,1,0:T(8,128)}), f32[16,16,1280]{2,1,0:T(8,128)S(1)}, u32[]{:S(2)}, u32[]{:S(2)}) %all-to-all-start.1) | async-done | bytes 1310752 | tf_op jit(solution)/shard_map/all_to_all | solution.py:464
  87.0 3.8 %all-to-all-start.2 = ((f32[16,16,1280]{2,1,0:T(8,128)}), f32[16,16,1280]{2,1,0:T(8,128)S(1)}, u32[]{:S(2)}, u32[]{:S(2)}) async-start(f32[16,16,1280]{2,1,0:T(8,128)} %copy-done.1), calls=%async_computation.2 | async-start | bytes 2621440 | tf_op jit(solution)/shard_map/all_to_all | solution.py:464
  91.5 17.2 %all-to-all-done.2 = f32[16,16,1280]{2,1,0:T(8,128)S(1)} async-done(((f32[16,16,1280]{2,1,0:T(8,128)}), f32[16,16,1280]{2,1,0:T(8,128)S(1)}, u32[]{:S(2)}, u32[]{:S(2)}) %all-to-all-start.2) | async-done | bytes 1310752 | tf_op jit(solution)/shard_map/all_to_all | solution.py:464
  108.7 3.4 %all-gather.6.cloned.1.call-done = bf16[256,48,384]{2,1,0:T(8,128)(2,1)} async-done(((bf16[16,48,384]{2,1,0:T(8,128)(2,1)}), bf16[256,48,384]{2,1,0:T(8,128)(2,1)}) %all-gather.6.cloned.1.call-update) | async-done | bytes 9437200 | tf_op jit(solution)/shard_map/all_gather | solution.py:488
  112.0 7.2 %shard_map.99 = bf16[16,3,64,256]{3,2,1,0:T(8,128)(2,1)} custom-call(f32[256,1280]{1,0:T(8,128)} %bitcast.13, f32[1,1280]{1,0:T(1,128)} %reshape.22.gain_ref, bf16[16,16,48,384]{3,2,1,0:T(8,128)(2,1)} %bitcast.15), custom_call_target="tpu_custom_call" | custom-call | flops 2013265920 | bytes 10485760 | tf_op jit(solution)/shard_map/pallas_call | solution.py:386
  119.2 9.9 %all-to-all-start.3 = ((bf16[16,3,64,256]{3,2,1,0:T(8,128)(2,1)}), bf16[16,3,64,256]{3,2,1,0:T(8,128)(2,1)S(1)}, u32[]{:S(2)}, u32[]{:S(2)}) async-start(bf16[16,3,64,256]{3,2,1,0:T(8,128)(2,1)} %shard_map.99), calls=%async_computation.3 | async-start | bytes 3145728 | tf_op jit(solution)/shard_map/all_to_all | solution.py:464
  129.7 37.9 %all-to-all-done.3.qkv_ref = bf16[16,3,64,256]{3,2,1,0:T(8,128)(2,1)S(1)} async-done(((bf16[16,3,64,256]{3,2,1,0:T(8,128)(2,1)}), bf16[16,3,64,256]{3,2,1,0:T(8,128)(2,1)S(1)}, u32[]{:S(2)}, u32[]{:S(2)}) %all-to-all-start.3) | async-done | bytes 1572896 | tf_op jit(solution)/shard_map/all_to_all | solution.py:464
  167.5 19.8 %shard_map.100 = bf16[16,64,256]{2,1,0:T(8,128)(2,1)} custom-call(bf16[16,3,64,256]{3,2,1,0:T(8,128)(2,1)S(1)} %all-to-all-done.3.qkv_ref), custom_call_target="tpu_custom_call" | custom-call | flops 17179869184 | bytes 3145728 | tf_op jit(solution)/shard_map/pallas_call | solution.py:71
  187.3 4.3 %all-to-all-start.4 = ((bf16[16,64,256]{2,1,0:T(8,128)(2,1)}), bf16[16,64,256]{2,1,0:T(8,128)(2,1)S(1)}, u32[]{:S(2)}, u32[]{:S(2)}) async-start(bf16[16,64,256]{2,1,0:T(8,128)(2,1)} %shard_map.100), calls=%async_computation.4 | async-start | bytes 1048576 | tf_op jit(solution)/shard_map/all_to_all | solution.py:464
  191.6 17.3 %all-to-all-done.4 = bf16[16,64,256]{2,1,0:T(8,128)(2,1)S(1)} async-done(((bf16[16,64,256]{2,1,0:T(8,128)(2,1)}), bf16[16,64,256]{2,1,0:T(8,128)(2,1)S(1)}, u32[]{:S(2)}, u32[]{:S(2)}) %all-to-all-start.4) | async-done | bytes 524320 | tf_op jit(solution)/shard_map/all_to_all | solution.py:464
  209.7 5.7 %shard_map.101 = (f32[256,1280]{1,0:T(8,128)}, f32[256,1280]{1,0:T(8,128)}) custom-call(bf16[1024,256]{1,0:T(8,128)(2,1)} %bitcast.19, bf16[1024,1280]{1,0:T(8,128)(2,1)} %all-gather.4.cloned.1.call-done.weight_ref, f32[256,1280]{1,0:T(8,128)} %bitcast.14), custom_call_target="tpu_custom_call" | custom-call | flops 671088640 | bytes 8388608 | tf_op jit(solution)/shard_map/pallas_call | solution.py:444
  (47 shorter events, 9.3 us)
Async XLA Ops:
  8.0 57.9 %copy-start = (f32[256,1280]{1,0:T(8,128)S(1)}, f32[256,1280]{1,0:T(8,128)}, u32[]{:S(2)}) copy-start(f32[256,1280]{1,0:T(8,128)} %param.9) | copy-start | bytes 3932164
  10.8 33.5 %all-to-all-start = ((bf16[16,96,640]{2,1,0:T(8,128)(2,1)}), bf16[16,96,640]{2,1,0:T(8,128)(2,1)S(1)}, u32[]{:S(2)}, u32[]{:S(2)}) async-start(bf16[16,96,640]{2,1,0:T(8,128)(2,1)} %get-tuple-element.24), calls=%async_computation | async-start | bytes 3932160 | tf_op jit(solution)/shard_map/all_to_all | solution.py:464
  18.4 93.6 %all-gather.6.cloned.1.call-start = ((), (), s32[]{:S(2)}) async-start(), calls=%async_computation.6 | async-start | bytes 10027008 | tf_op jit(solution)/shard_map/all_gather | solution.py:488
  18.4 13.4 %collective-permute-start = (bf16[64,512]{1,0:T(8,128)(2,1)}, bf16[64,512]{1,0:T(8,128)(2,1)S(1)}, u32[]{:S(2)}, u32[]{:S(2)}) collective-permute-start(bf16[64,512]{1,0:T(8,128)(2,1)} %get-tuple-element.17), channel_id=1, source_target_pairs={{0,2},{1,3},{2,4},{3,5},{4,6},{5,7},{6,8},{7,9},{8,10},{9,11},{10,... | collective-permute-start | bytes 196616 | tf_op jit(solution)/shard_map/ppermute | solution.py:484
  20.2 14.1 %collective-permute-start.1 = (bf16[64,512]{1,0:T(8,128)(2,1)}, bf16[64,512]{1,0:T(8,128)(2,1)S(1)}, u32[]{:S(2)}, u32[]{:S(2)}) collective-permute-start(bf16[64,512]{1,0:T(8,128)(2,1)} %get-tuple-element.18), channel_id=1, source_target_pairs={{0,4},{1,5},{2,6},{3,7},{4,8},{5,9},{6,10},{7,11},{8,12},{9,13},{1... | collective-permute-start | bytes 196616 | tf_op jit(solution)/shard_map/ppermute | solution.py:484
  23.2 11.8 %collective-permute-start.2 = (bf16[64,512]{1,0:T(8,128)(2,1)}, bf16[64,512]{1,0:T(8,128)(2,1)S(1)}, u32[]{:S(2)}, u32[]{:S(2)}) collective-permute-start(bf16[64,512]{1,0:T(8,128)(2,1)} %get-tuple-element.19), channel_id=1, source_target_pairs={{0,6},{1,7},{2,8},{3,9},{4,10},{5,11},{6,12},{7,13},{8,14},{9,15},... | collective-permute-start | bytes 196616 | tf_op jit(solution)/shard_map/ppermute | solution.py:484
  26.9 8.1 %collective-permute-start.3 = (bf16[64,512]{1,0:T(8,128)(2,1)}, bf16[64,512]{1,0:T(8,128)(2,1)S(1)}, u32[]{:S(2)}, u32[]{:S(2)}) collective-permute-start(bf16[64,512]{1,0:T(8,128)(2,1)} %get-tuple-element.20), channel_id=1, source_target_pairs={{0,8},{1,9},{2,10},{3,11},{4,12},{5,13},{6,14},{7,15},{8,0},{9,1},... | collective-permute-start | bytes 196616 | tf_op jit(solution)/shard_map/ppermute | solution.py:484
  27.4 7.6 %collective-permute-start.4 = (bf16[64,512]{1,0:T(8,128)(2,1)}, bf16[64,512]{1,0:T(8,128)(2,1)S(1)}, u32[]{:S(2)}, u32[]{:S(2)}) collective-permute-start(bf16[64,512]{1,0:T(8,128)(2,1)} %get-tuple-element.21), channel_id=1, source_target_pairs={{0,10},{1,11},{2,12},{3,13},{4,14},{5,15},{6,0},{7,1},{8,2},{9,3},... | collective-permute-start | bytes 196616 | tf_op jit(solution)/shard_map/ppermute | solution.py:484
  31.8 12.4 %copy-start.7 = (bf16[64,512]{1,0:T(8,128)(2,1)}, bf16[64,512]{1,0:T(8,128)(2,1)S(1)}, u32[]{:S(2)}) copy-start(bf16[64,512]{1,0:T(8,128)(2,1)S(1)} %collective-permute-done.refs_0_) | copy-start | bytes 196612
  31.8 10.4 %collective-permute-start.5 = (bf16[64,512]{1,0:T(8,128)(2,1)}, bf16[64,512]{1,0:T(8,128)(2,1)S(1)}, u32[]{:S(2)}, u32[]{:S(2)}) collective-permute-start(bf16[64,512]{1,0:T(8,128)(2,1)} %get-tuple-element.22), channel_id=1, source_target_pairs={{0,12},{1,13},{2,14},{3,15},{4,0},{5,1},{6,2},{7,3},{8,4},{9,5},{1... | collective-permute-start | bytes 196616 | tf_op jit(solution)/shard_map/ppermute | solution.py:484
  34.2 10.0 %copy-start.8 = (bf16[64,512]{1,0:T(8,128)(2,1)}, bf16[64,512]{1,0:T(8,128)(2,1)S(1)}, u32[]{:S(2)}) copy-start(bf16[64,512]{1,0:T(8,128)(2,1)S(1)} %collective-permute-done.1.refs_1_) | copy-start | bytes 196612
  34.2 8.6 %collective-permute-start.6 = (bf16[64,512]{1,0:T(8,128)(2,1)}, bf16[64,512]{1,0:T(8,128)(2,1)}, u32[]{:S(2)}, u32[]{:S(2)}) collective-permute-start(bf16[64,512]{1,0:T(8,128)(2,1)} %get-tuple-element.23), channel_id=1, source_target_pairs={{0,14},{1,15},{2,0},{3,1},{4,2},{5,3},{6,4},{7,5},{8,6},{9,7},{10,... | collective-permute-start | bytes 196616 | tf_op jit(solution)/shard_map/ppermute | solution.py:484
  35.0 9.3 %copy-start.9 = (bf16[64,512]{1,0:T(8,128)(2,1)}, bf16[64,512]{1,0:T(8,128)(2,1)S(1)}, u32[]{:S(2)}) copy-start(bf16[64,512]{1,0:T(8,128)(2,1)S(1)} %collective-permute-done.2.refs_2_) | copy-start | bytes 196612
  35.0 9.3 %copy-start.10 = (bf16[64,512]{1,0:T(8,128)(2,1)}, bf16[64,512]{1,0:T(8,128)(2,1)S(1)}, u32[]{:S(2)}) copy-start(bf16[64,512]{1,0:T(8,128)(2,1)S(1)} %collective-permute-done.3.refs_3_) | copy-start | bytes 196612
  35.0 7.2 %copy-start.11 = (bf16[64,512]{1,0:T(8,128)(2,1)}, bf16[64,512]{1,0:T(8,128)(2,1)S(1)}, u32[]{:S(2)}) copy-start(bf16[64,512]{1,0:T(8,128)(2,1)S(1)} %collective-permute-done.4.refs_4_) | copy-start | bytes 196612
  47.9 8.1 %collective-permute-start.8 = (bf16[16,96,640]{2,1,0:T(8,128)(2,1)}, bf16[16,96,640]{2,1,0:T(8,128)(2,1)S(1)}, u32[]{:S(2)}, u32[]{:S(2)}) collective-permute-start(bf16[16,96,640]{2,1,0:T(8,128)(2,1)} %get-tuple-element.27.mine_ref), channel_id=1, source_target_pairs={{0,1},{1,0},{2,3},{3,2},{4,5},{5,4},{6,7},{7,6},{8,9},{9,8},{10,11... | collective-permute-start | bytes 5898248 | tf_op jit(solution)/shard_map/ppermute | solution.py:490
  51.7 4.2 %collective-permute-start.7 = (bf16[8,64,256]{2,1,0:T(8,128)(2,1)}, bf16[8,64,256]{2,1,0:T(8,128)(2,1)S(1)}, u32[]{:S(2)}, u32[]{:S(2)}) collective-permute-start(bf16[8,64,256]{2,1,0:T(8,128)(2,1)} %get-tuple-element.26), channel_id=1, source_target_pairs={{0,1},{1,0},{2,3},{3,2},{4,5},{5,4},{6,7},{7,6},{8,9},{9,8},{10,11... | collective-permute-start | bytes 786440 | tf_op jit(solution)/shard_map/ppermute | solution.py:489
  62.2 23.7 %all-to-all-start.1 = ((f32[16,16,1280]{2,1,0:T(8,128)}), f32[16,16,1280]{2,1,0:T(8,128)S(1)}, u32[]{:S(2)}, u32[]{:S(2)}) async-start(f32[16,16,1280]{2,1,0:T(8,128)} %bitcast.16), calls=%async_computation.1 | async-start | bytes 2621440 | tf_op jit(solution)/shard_map/all_to_all | solution.py:464
  87.0 3.8 %copy-start.13 = (f32[1280]{0:T(1024)S(1)}, f32[1280]{0:T(1024)}, u32[]{:S(2)}) copy-start(f32[1280]{0:T(1024)} %param.15) | copy-start | bytes 15364
  87.0 21.6 %all-to-all-start.2 = ((f32[16,16,1280]{2,1,0:T(8,128)}), f32[16,16,1280]{2,1,0:T(8,128)S(1)}, u32[]{:S(2)}, u32[]{:S(2)}) async-start(f32[16,16,1280]{2,1,0:T(8,128)} %copy-done.1), calls=%async_computation.2 | async-start | bytes 2621440 | tf_op jit(solution)/shard_map/all_to_all | solution.py:464
  108.6 3.4 %copy-start.3 = (f32[16,16,1280]{2,1,0:T(8,128)}, f32[16,16,1280]{2,1,0:T(8,128)S(1)}, u32[]{:S(2)}) copy-start(f32[16,16,1280]{2,1,0:T(8,128)S(1)} %all-to-all-done.2) | copy-start | bytes 3932164
  119.2 48.3 %all-to-all-start.3 = ((bf16[16,3,64,256]{3,2,1,0:T(8,128)(2,1)}), bf16[16,3,64,256]{3,2,1,0:T(8,128)(2,1)S(1)}, u32[]{:S(2)}, u32[]{:S(2)}) async-start(bf16[16,3,64,256]{3,2,1,0:T(8,128)(2,1)} %shard_map.99), calls=%async_computation.3 | async-start | bytes 3145728 | tf_op jit(solution)/shard_map/all_to_all | solution.py:464
  129.1 62.5 %all-gather.4.cloned.1.call-start = ((), (), s32[]{:S(2)}) async-start(), calls=%async_computation.5 | async-start | bytes 2785280 | tf_op jit(solution)/shard_map/all_gather | solution.py:498
  187.3 21.6 %all-to-all-start.4 = ((bf16[16,64,256]{2,1,0:T(8,128)(2,1)}), bf16[16,64,256]{2,1,0:T(8,128)(2,1)S(1)}, u32[]{:S(2)}, u32[]{:S(2)}) async-start(bf16[16,64,256]{2,1,0:T(8,128)(2,1)} %shard_map.100), calls=%async_computation.4 | async-start | bytes 1048576 | tf_op jit(solution)/shard_map/all_to_all | solution.py:464
  (6 other events, 5.9 us)
Sparse Core Ops, SparseCore 0:
  48.0 64.0 all-gather.5
Sparse Core Ops, SparseCore 1:
  132.1 47.7 all-gather.3
where the time goes:
time: 224 us; the launch traced here: 223 us
  waiting for transfers between devices  109 us (49%)
  starting transfers between devices  49.9 us (22%)
  Pallas kernels  42.6 us (19%)
  between operations  15.7 us (7%)
  local copies, waits for them, and re-layouts  5.84 us (3%)
    all_to_all x5, waiting for transfers between devices, swap(): return lax.all_to_all(blocks, axis, split_axis=0, concat_axis=0, tiled=True)  93.7 us
    all_to_all x5, starting transfers between devices, swap(): return lax.all_to_all(blocks, axis, split_axis=0, concat_axis=0, tiled=True)  29.3 us
    pallas_call x1, Pallas kernels, attend(): pl.pallas_call(attention_kernel, out_shape=jax.ShapeDtypeStruct((blocks,...  19.8 us
    ppermute x7, starting transfers between devices, local(): lax.ppermute(piece, 'seq', [(i, (i + 2 * k + 2) % seqs) for i in range(se...  16.5 us
    ppermute x7, waiting for transfers between devices, local(): lax.ppermute(piece, 'seq', [(i, (i + 2 * k + 2) % seqs) for i in range(se...  7.23 us
    pallas_call x1, Pallas kernels, project_qkv(): pl.pallas_call(qkv_kernel, out_shape=jax.ShapeDtypeStruct(shape, jnp.bflo...  7.18 us
    pallas_call x1, Pallas kernels, mix(): pl.pallas_call(mix_kernel, out_shape=(jax.ShapeDtypeStruct(advanced.shape...  5.73 us
    unnamed x28, local copies, waits for them, and re-layouts  5.23 us
  transfers between devices with their start and end apart: 16, of which 8 were waited for; matrix products, arithmetic and copies ran while one was open for 0% of the time, Pallas kernels for 11%

commit v1 on v0

--- a/solution.py
+++ b/solution.py
@@ -341,10 +341,13 @@
                 ),
             )
         )
-    for pair in loads[:4]:
+    for pair in loads[:2]:
         for load in pair:
             load.start()
     load_rows.wait()
+    for pair in loads[2:4]:
+        for load in pair:
+            load.start()
     gain = gain_ref[...]
     part_rows = 32
     for first in range(0, rows, part_rows):
@@ -415,9 +418,11 @@
         pltpu.make_async_copy(weight_ref.at[:, b * wide : (b + 1) * wide], weight.at[b], done.at[b])
         for b in range(chunks)
     ]
-    for load in (*loads, load_advanced):
+    for load in (loads[0], load_advanced):
         load.start()
     token_rows = attended_ref[...].T
+    for load in loads[1:]:
+        load.start()
     stores = []
     for b in range(chunks):
         columns = slice(b * wide, (b + 1) * wide)

time: 224 us -> 223 us (level)
  no operation moved by 1% of the time
where the time goes in v1:
time: 223 us; the launch traced here: 222 us
  waiting for transfers between devices  109 us (49%)
  starting transfers between devices  49.9 us (22%)
  Pallas kernels  42.1 us (19%)
  between operations  15.7 us (7%)
  local copies, waits for them, and re-layouts  5.84 us (3%)
    all_to_all x5, waiting for transfers between devices, swap(): return lax.all_to_all(blocks, axis, split_axis=0, concat_axis=0, tiled=True)  93.7 us
    all_to_all x5, starting transfers between devices, swap(): return lax.all_to_all(blocks, axis, split_axis=0, concat_axis=0, tiled=True)  29.3 us
    pallas_call x1, Pallas kernels, attend(): pl.pallas_call(attention_kernel, out_shape=jax.ShapeDtypeStruct((blocks,...  19.8 us
    ppermute x7, starting transfers between devices, local(): lax.ppermute(piece, 'seq', [(i, (i + 2 * k + 2) % seqs) for i in range(se...  16.5 us
    pallas_call x1, Pallas kernels, project_qkv(): pl.pallas_call(qkv_kernel, out_shape=jax.ShapeDtypeStruct(shape, jnp.bflo...  7.3 us
    ppermute x7, waiting for transfers between devices, local(): lax.ppermute(piece, 'seq', [(i, (i + 2 * k + 2) % seqs) for i in range(se...  7.23 us
    unnamed x28, local copies, waits for them, and re-layouts  5.23 us
    pallas_call x1, Pallas kernels, mix(): pl.pallas_call(mix_kernel, out_shape=(jax.ShapeDtypeStruct(advanced.shape...  5.15 us
  transfers between devices with their start and end apart: 16, of which 8 were waited for; matrix products, arithmetic and copies ran while one was open for 0% of the time, Pallas kernels for 11%

profile of v1, /device:TPU:1, one launch (start us, length us, event | category | flops | bytes accessed | tf_op | source)
XLA Modules:
  0.0 222.5 jit_solution(18404286064652286636)
XLA Ops:
  8.0 2.8 %shard_map.95 = (bf16[16,96,640]{2,1,0:T(8,128)(2,1)}, bf16[64,1280]{1,0:T(8,128)(2,1)}, bf16[64,512]{1,0:T(8,128)(2,1)}, bf16[64,512]{1,0:T(8,128)(2,1)}, bf16[...) custom-call(s32[1]{0:T(128)} %bitcast.seq_ref, ...), custom_call_target="tpu_custom_call" | custom-call | bytes 4194304 | tf_op jit(solution)/shard_map/pallas_call | solution.py:152
  10.8 7.6 %all-to-all-start = ((bf16[16,96,640]{2,1,0:T(8,128)(2,1)}), bf16[16,96,640]{2,1,0:T(8,128)(2,1)S(1)}, u32[]{:S(2)}, u32[]{:S(2)}) async-start(bf16[16,96,640]{2,1,0:T(8,128)(2,1)} %get-tuple-element.24), calls=%async_computation | async-start | bytes 3932160 | tf_op jit(solution)/shard_map/all_to_all | solution.py:469
  18.4 1.7 collective-permute-start
  20.2 3.0 %collective-permute-start.1 = (bf16[64,512]{1,0:T(8,128)(2,1)}, bf16[64,512]{1,0:T(8,128)(2,1)S(1)}, u32[]{:S(2)}, u32[]{:S(2)}) collective-permute-start(bf16[64,512]{1,0:T(8,128)(2,1)} %get-tuple-element.18), channel_id=1, source_target_pairs={{0,4},{1,5},{2,6},{3,7},{4,8},{5,9},{6,10},{7,11},{8,12},{9,13},{1... | collective-permute-start | bytes 196616 | tf_op jit(solution)/shard_map/ppermute | solution.py:489
  23.2 3.8 %collective-permute-start.2 = (bf16[64,512]{1,0:T(8,128)(2,1)}, bf16[64,512]{1,0:T(8,128)(2,1)S(1)}, u32[]{:S(2)}, u32[]{:S(2)}) collective-permute-start(bf16[64,512]{1,0:T(8,128)(2,1)} %get-tuple-element.19), channel_id=1, source_target_pairs={{0,6},{1,7},{2,8},{3,9},{4,10},{5,11},{6,12},{7,13},{8,14},{9,15},... | collective-permute-start | bytes 196616 | tf_op jit(solution)/shard_map/ppermute | solution.py:489
  27.4 4.5 %collective-permute-start.4 = (bf16[64,512]{1,0:T(8,128)(2,1)}, bf16[64,512]{1,0:T(8,128)(2,1)S(1)}, u32[]{:S(2)}, u32[]{:S(2)}) collective-permute-start(bf16[64,512]{1,0:T(8,128)(2,1)} %get-tuple-element.21), channel_id=1, source_target_pairs={{0,10},{1,11},{2,12},{3,13},{4,14},{5,15},{6,0},{7,1},{8,2},{9,3},... | collective-permute-start | bytes 196616 | tf_op jit(solution)/shard_map/ppermute | solution.py:489
  31.8 2.4 %collective-permute-start.5 = (bf16[64,512]{1,0:T(8,128)(2,1)}, bf16[64,512]{1,0:T(8,128)(2,1)S(1)}, u32[]{:S(2)}, u32[]{:S(2)}) collective-permute-start(bf16[64,512]{1,0:T(8,128)(2,1)} %get-tuple-element.22), channel_id=1, source_target_pairs={{0,12},{1,13},{2,14},{3,15},{4,0},{5,1},{6,2},{7,3},{8,4},{9,5},{1... | collective-permute-start | bytes 196616 | tf_op jit(solution)/shard_map/ppermute | solution.py:489
  35.0 7.2 %collective-permute-done.5.refs_5_ = bf16[64,512]{1,0:T(8,128)(2,1)S(1)} collective-permute-done((bf16[64,512]{1,0:T(8,128)(2,1)}, bf16[64,512]{1,0:T(8,128)(2,1)S(1)}, u32[]{:S(2)}, u32[]{:S(2)}) %collective-permute-start.5) | collective-permute-done | bytes 65568 | tf_op jit(solution)/shard_map/ppermute | solution.py:489
  45.6 2.3 %shard_map.96 = (bf16[8,64,256]{2,1,0:T(8,128)(2,1)}, bf16[8,64,256]{2,1,0:T(8,128)(2,1)}, bf16[16,48,384]{2,1,0:T(8,128)(2,1)}, bf16[16,96,640]{2,1,0:T(8,128)(2,1)}) custom-call(s32[1]{0:T(128)} %bitcast.seq_ref, bf16[64,4096]{1,0:T(8,128)(2,1)} %bitcast.18, bf16[64,512]{1,0:T(8,128)(2,1)} %copy-done.7, ...), custom_call_target="tpu_custom_call", output_to_operand_aliasing={{3}: (9, {})} | custom-call | bytes 1048576 | tf_op jit(solution)/shard_map/pallas_call | solution.py:211
  47.9 3.9 %collective-permute-start.8 = (bf16[16,96,640]{2,1,0:T(8,128)(2,1)}, bf16[16,96,640]{2,1,0:T(8,128)(2,1)S(1)}, u32[]{:S(2)}, u32[]{:S(2)}) collective-permute-start(bf16[16,96,640]{2,1,0:T(8,128)(2,1)} %get-tuple-element.27.mine_ref), channel_id=1, source_target_pairs={{0,1},{1,0},{2,3},{3,2},{4,5},{5,4},{6,7},{7,6},{8,9},{9,8},{10,11... | collective-permute-start | bytes 5898248 | tf_op jit(solution)/shard_map/ppermute | solution.py:495
  51.8 4.1 %collective-permute-done.7.taken_ref = bf16[8,64,256]{2,1,0:T(8,128)(2,1)S(1)} collective-permute-done((bf16[8,64,256]{2,1,0:T(8,128)(2,1)}, bf16[8,64,256]{2,1,0:T(8,128)(2,1)S(1)}, u32[]{:S(2)}, u32[]{:S(2)}) %collective-permute-start.7) | collective-permute-done | bytes 262176 | tf_op jit(solution)/shard_map/ppermute | solution.py:494
  57.4 4.8 %shard_map.97 = f32[256,1280]{1,0:T(8,128)} custom-call(s32[1]{0:T(128)} %bitcast.seq_ref, f32[3]{0:T(128)} %bitcast.22, bf16[8,64,256]{2,1,0:T(8,128)(2,1)} %get-tuple-element.25.kept_ref, bf16[8,64,256]{2,1,0:T(8,128)(2,1)} %copy-done.6, bf16[16,96,640]{2,1,0:T(8,128)(2,1)} %get-tuple-element.27.mine_ref, bf16[16,96,640]{2,1,0:T(8,128)(2,1)} %copy-done.5, ...), custom_call_target="tpu_custom_call" | custom-call | flops 671088640 | bytes 8388608 | tf_op jit(solution)/shard_map/pallas_call | solution.py:278
  62.2 3.7 %all-to-all-start.1 = ((f32[16,16,1280]{2,1,0:T(8,128)}), f32[16,16,1280]{2,1,0:T(8,128)S(1)}, u32[]{:S(2)}, u32[]{:S(2)}) async-start(f32[16,16,1280]{2,1,0:T(8,128)} %bitcast.16), calls=%async_computation.1 | async-start | bytes 2621440 | tf_op jit(solution)/shard_map/all_to_all | solution.py:469
  65.9 20.0 %all-to-all-done.1.drifts_ref = f32[16,16,1280]{2,1,0:T(8,128)S(1)} async-done(((f32[16,16,1280]{2,1,0:T(8,128)}), f32[16,16,1280]{2,1,0:T(8,128)S(1)}, u32[]{:S(2)}, u32[]{:S(2)}) %all-to-all-start.1) | async-done | bytes 1310752 | tf_op jit(solution)/shard_map/all_to_all | solution.py:469
  87.0 3.8 %all-to-all-start.2 = ((f32[16,16,1280]{2,1,0:T(8,128)}), f32[16,16,1280]{2,1,0:T(8,128)S(1)}, u32[]{:S(2)}, u32[]{:S(2)}) async-start(f32[16,16,1280]{2,1,0:T(8,128)} %copy-done.1), calls=%async_computation.2 | async-start | bytes 2621440 | tf_op jit(solution)/shard_map/all_to_all | solution.py:469
  91.5 17.2 %all-to-all-done.2 = f32[16,16,1280]{2,1,0:T(8,128)S(1)} async-done(((f32[16,16,1280]{2,1,0:T(8,128)}), f32[16,16,1280]{2,1,0:T(8,128)S(1)}, u32[]{:S(2)}, u32[]{:S(2)}) %all-to-all-start.2) | async-done | bytes 1310752 | tf_op jit(solution)/shard_map/all_to_all | solution.py:469
  108.7 3.4 %all-gather.6.cloned.1.call-done = bf16[256,48,384]{2,1,0:T(8,128)(2,1)} async-done(((bf16[16,48,384]{2,1,0:T(8,128)(2,1)}), bf16[256,48,384]{2,1,0:T(8,128)(2,1)}) %all-gather.6.cloned.1.call-update) | async-done | bytes 9437200 | tf_op jit(solution)/shard_map/all_gather | solution.py:493
  112.0 7.3 %shard_map.99 = bf16[16,3,64,256]{3,2,1,0:T(8,128)(2,1)} custom-call(f32[256,1280]{1,0:T(8,128)} %bitcast.13, f32[1,1280]{1,0:T(1,128)} %reshape.22.gain_ref, bf16[16,16,48,384]{3,2,1,0:T(8,128)(2,1)} %bitcast.15), custom_call_target="tpu_custom_call" | custom-call | flops 2013265920 | bytes 10485760 | tf_op jit(solution)/shard_map/pallas_call | solution.py:389
  119.4 9.9 %all-to-all-start.3 = ((bf16[16,3,64,256]{3,2,1,0:T(8,128)(2,1)}), bf16[16,3,64,256]{3,2,1,0:T(8,128)(2,1)S(1)}, u32[]{:S(2)}, u32[]{:S(2)}) async-start(bf16[16,3,64,256]{3,2,1,0:T(8,128)(2,1)} %shard_map.99), calls=%async_computation.3 | async-start | bytes 3145728 | tf_op jit(solution)/shard_map/all_to_all | solution.py:469
  129.8 37.9 %all-to-all-done.3.qkv_ref = bf16[16,3,64,256]{3,2,1,0:T(8,128)(2,1)S(1)} async-done(((bf16[16,3,64,256]{3,2,1,0:T(8,128)(2,1)}), bf16[16,3,64,256]{3,2,1,0:T(8,128)(2,1)S(1)}, u32[]{:S(2)}, u32[]{:S(2)}) %all-to-all-start.3) | async-done | bytes 1572896 | tf_op jit(solution)/shard_map/all_to_all | solution.py:469
  167.7 19.8 %shard_map.100 = bf16[16,64,256]{2,1,0:T(8,128)(2,1)} custom-call(bf16[16,3,64,256]{3,2,1,0:T(8,128)(2,1)S(1)} %all-to-all-done.3.qkv_ref), custom_call_target="tpu_custom_call" | custom-call | flops 17179869184 | bytes 3145728 | tf_op jit(solution)/shard_map/pallas_call | solution.py:71
  187.5 4.3 %all-to-all-start.4 = ((bf16[16,64,256]{2,1,0:T(8,128)(2,1)}), bf16[16,64,256]{2,1,0:T(8,128)(2,1)S(1)}, u32[]{:S(2)}, u32[]{:S(2)}) async-start(bf16[16,64,256]{2,1,0:T(8,128)(2,1)} %shard_map.100), calls=%async_computation.4 | async-start | bytes 1048576 | tf_op jit(solution)/shard_map/all_to_all | solution.py:469
  191.8 17.3 %all-to-all-done.4 = bf16[16,64,256]{2,1,0:T(8,128)(2,1)S(1)} async-done(((bf16[16,64,256]{2,1,0:T(8,128)(2,1)}), bf16[16,64,256]{2,1,0:T(8,128)(2,1)S(1)}, u32[]{:S(2)}, u32[]{:S(2)}) %all-to-all-start.4) | async-done | bytes 524320 | tf_op jit(solution)/shard_map/all_to_all | solution.py:469
  209.9 5.1 %shard_map.101 = (f32[256,1280]{1,0:T(8,128)}, f32[256,1280]{1,0:T(8,128)}) custom-call(bf16[1024,256]{1,0:T(8,128)(2,1)} %bitcast.19, bf16[1024,1280]{1,0:T(8,128)(2,1)} %all-gather.4.cloned.1.call-done.weight_ref, f32[256,1280]{1,0:T(8,128)} %bitcast.14), custom_call_target="tpu_custom_call" | custom-call | flops 671088640 | bytes 8388608 | tf_op jit(solution)/shard_map/pallas_call | solution.py:449
  (47 shorter events, 9.3 us)
Async XLA Ops:
  8.0 57.9 %copy-start = (f32[256,1280]{1,0:T(8,128)S(1)}, f32[256,1280]{1,0:T(8,128)}, u32[]{:S(2)}) copy-start(f32[256,1280]{1,0:T(8,128)} %param.9) | copy-start | bytes 3932164
  10.8 33.5 %all-to-all-start = ((bf16[16,96,640]{2,1,0:T(8,128)(2,1)}), bf16[16,96,640]{2,1,0:T(8,128)(2,1)S(1)}, u32[]{:S(2)}, u32[]{:S(2)}) async-start(bf16[16,96,640]{2,1,0:T(8,128)(2,1)} %get-tuple-element.24), calls=%async_computation | async-start | bytes 3932160 | tf_op jit(solution)/shard_map/all_to_all | solution.py:469
  18.4 93.6 %all-gather.6.cloned.1.call-start = ((), (), s32[]{:S(2)}) async-start(), calls=%async_computation.6 | async-start | bytes 10027008 | tf_op jit(solution)/shard_map/all_gather | solution.py:493
  18.4 13.4 %collective-permute-start = (bf16[64,512]{1,0:T(8,128)(2,1)}, bf16[64,512]{1,0:T(8,128)(2,1)S(1)}, u32[]{:S(2)}, u32[]{:S(2)}) collective-permute-start(bf16[64,512]{1,0:T(8,128)(2,1)} %get-tuple-element.17), channel_id=1, source_target_pairs={{0,2},{1,3},{2,4},{3,5},{4,6},{5,7},{6,8},{7,9},{8,10},{9,11},{10,... | collective-permute-start | bytes 196616 | tf_op jit(solution)/shard_map/ppermute | solution.py:489
  20.2 14.1 %collective-permute-start.1 = (bf16[64,512]{1,0:T(8,128)(2,1)}, bf16[64,512]{1,0:T(8,128)(2,1)S(1)}, u32[]{:S(2)}, u32[]{:S(2)}) collective-permute-start(bf16[64,512]{1,0:T(8,128)(2,1)} %get-tuple-element.18), channel_id=1, source_target_pairs={{0,4},{1,5},{2,6},{3,7},{4,8},{5,9},{6,10},{7,11},{8,12},{9,13},{1... | collective-permute-start | bytes 196616 | tf_op jit(solution)/shard_map/ppermute | solution.py:489
  23.2 11.8 %collective-permute-start.2 = (bf16[64,512]{1,0:T(8,128)(2,1)}, bf16[64,512]{1,0:T(8,128)(2,1)S(1)}, u32[]{:S(2)}, u32[]{:S(2)}) collective-permute-start(bf16[64,512]{1,0:T(8,128)(2,1)} %get-tuple-element.19), channel_id=1, source_target_pairs={{0,6},{1,7},{2,8},{3,9},{4,10},{5,11},{6,12},{7,13},{8,14},{9,15},... | collective-permute-start | bytes 196616 | tf_op jit(solution)/shard_map/ppermute | solution.py:489
  26.9 8.1 %collective-permute-start.3 = (bf16[64,512]{1,0:T(8,128)(2,1)}, bf16[64,512]{1,0:T(8,128)(2,1)S(1)}, u32[]{:S(2)}, u32[]{:S(2)}) collective-permute-start(bf16[64,512]{1,0:T(8,128)(2,1)} %get-tuple-element.20), channel_id=1, source_target_pairs={{0,8},{1,9},{2,10},{3,11},{4,12},{5,13},{6,14},{7,15},{8,0},{9,1},... | collective-permute-start | bytes 196616 | tf_op jit(solution)/shard_map/ppermute | solution.py:489
  27.4 7.6 %collective-permute-start.4 = (bf16[64,512]{1,0:T(8,128)(2,1)}, bf16[64,512]{1,0:T(8,128)(2,1)S(1)}, u32[]{:S(2)}, u32[]{:S(2)}) collective-permute-start(bf16[64,512]{1,0:T(8,128)(2,1)} %get-tuple-element.21), channel_id=1, source_target_pairs={{0,10},{1,11},{2,12},{3,13},{4,14},{5,15},{6,0},{7,1},{8,2},{9,3},... | collective-permute-start | bytes 196616 | tf_op jit(solution)/shard_map/ppermute | solution.py:489
  31.8 12.4 %copy-start.7 = (bf16[64,512]{1,0:T(8,128)(2,1)}, bf16[64,512]{1,0:T(8,128)(2,1)S(1)}, u32[]{:S(2)}) copy-start(bf16[64,512]{1,0:T(8,128)(2,1)S(1)} %collective-permute-done.refs_0_) | copy-start | bytes 196612
  31.8 10.4 %collective-permute-start.5 = (bf16[64,512]{1,0:T(8,128)(2,1)}, bf16[64,512]{1,0:T(8,128)(2,1)S(1)}, u32[]{:S(2)}, u32[]{:S(2)}) collective-permute-start(bf16[64,512]{1,0:T(8,128)(2,1)} %get-tuple-element.22), channel_id=1, source_target_pairs={{0,12},{1,13},{2,14},{3,15},{4,0},{5,1},{6,2},{7,3},{8,4},{9,5},{1... | collective-permute-start | bytes 196616 | tf_op jit(solution)/shard_map/ppermute | solution.py:489
  34.2 10.0 %copy-start.8 = (bf16[64,512]{1,0:T(8,128)(2,1)}, bf16[64,512]{1,0:T(8,128)(2,1)S(1)}, u32[]{:S(2)}) copy-start(bf16[64,512]{1,0:T(8,128)(2,1)S(1)} %collective-permute-done.1.refs_1_) | copy-start | bytes 196612
  34.2 8.6 %collective-permute-start.6 = (bf16[64,512]{1,0:T(8,128)(2,1)}, bf16[64,512]{1,0:T(8,128)(2,1)}, u32[]{:S(2)}, u32[]{:S(2)}) collective-permute-start(bf16[64,512]{1,0:T(8,128)(2,1)} %get-tuple-element.23), channel_id=1, source_target_pairs={{0,14},{1,15},{2,0},{3,1},{4,2},{5,3},{6,4},{7,5},{8,6},{9,7},{10,... | collective-permute-start | bytes 196616 | tf_op jit(solution)/shard_map/ppermute | solution.py:489
  35.0 9.3 %copy-start.9 = (bf16[64,512]{1,0:T(8,128)(2,1)}, bf16[64,512]{1,0:T(8,128)(2,1)S(1)}, u32[]{:S(2)}) copy-start(bf16[64,512]{1,0:T(8,128)(2,1)S(1)} %collective-permute-done.2.refs_2_) | copy-start | bytes 196612
  35.0 9.3 %copy-start.10 = (bf16[64,512]{1,0:T(8,128)(2,1)}, bf16[64,512]{1,0:T(8,128)(2,1)S(1)}, u32[]{:S(2)}) copy-start(bf16[64,512]{1,0:T(8,128)(2,1)S(1)} %collective-permute-done.3.refs_3_) | copy-start | bytes 196612
  35.0 7.2 %copy-start.11 = (bf16[64,512]{1,0:T(8,128)(2,1)}, bf16[64,512]{1,0:T(8,128)(2,1)S(1)}, u32[]{:S(2)}) copy-start(bf16[64,512]{1,0:T(8,128)(2,1)S(1)} %collective-permute-done.4.refs_4_) | copy-start | bytes 196612
  47.9 8.1 %collective-permute-start.8 = (bf16[16,96,640]{2,1,0:T(8,128)(2,1)}, bf16[16,96,640]{2,1,0:T(8,128)(2,1)S(1)}, u32[]{:S(2)}, u32[]{:S(2)}) collective-permute-start(bf16[16,96,640]{2,1,0:T(8,128)(2,1)} %get-tuple-element.27.mine_ref), channel_id=1, source_target_pairs={{0,1},{1,0},{2,3},{3,2},{4,5},{5,4},{6,7},{7,6},{8,9},{9,8},{10,11... | collective-permute-start | bytes 5898248 | tf_op jit(solution)/shard_map/ppermute | solution.py:495
  51.7 4.2 %collective-permute-start.7 = (bf16[8,64,256]{2,1,0:T(8,128)(2,1)}, bf16[8,64,256]{2,1,0:T(8,128)(2,1)S(1)}, u32[]{:S(2)}, u32[]{:S(2)}) collective-permute-start(bf16[8,64,256]{2,1,0:T(8,128)(2,1)} %get-tuple-element.26), channel_id=1, source_target_pairs={{0,1},{1,0},{2,3},{3,2},{4,5},{5,4},{6,7},{7,6},{8,9},{9,8},{10,11... | collective-permute-start | bytes 786440 | tf_op jit(solution)/shard_map/ppermute | solution.py:494
  62.2 23.7 %all-to-all-start.1 = ((f32[16,16,1280]{2,1,0:T(8,128)}), f32[16,16,1280]{2,1,0:T(8,128)S(1)}, u32[]{:S(2)}, u32[]{:S(2)}) async-start(f32[16,16,1280]{2,1,0:T(8,128)} %bitcast.16), calls=%async_computation.1 | async-start | bytes 2621440 | tf_op jit(solution)/shard_map/all_to_all | solution.py:469
  87.0 3.8 %copy-start.13 = (f32[1280]{0:T(1024)S(1)}, f32[1280]{0:T(1024)}, u32[]{:S(2)}) copy-start(f32[1280]{0:T(1024)} %param.15) | copy-start | bytes 15364
  87.0 21.6 %all-to-all-start.2 = ((f32[16,16,1280]{2,1,0:T(8,128)}), f32[16,16,1280]{2,1,0:T(8,128)S(1)}, u32[]{:S(2)}, u32[]{:S(2)}) async-start(f32[16,16,1280]{2,1,0:T(8,128)} %copy-done.1), calls=%async_computation.2 | async-start | bytes 2621440 | tf_op jit(solution)/shard_map/all_to_all | solution.py:469
  108.6 3.4 %copy-start.3 = (f32[16,16,1280]{2,1,0:T(8,128)}, f32[16,16,1280]{2,1,0:T(8,128)S(1)}, u32[]{:S(2)}) copy-start(f32[16,16,1280]{2,1,0:T(8,128)S(1)} %all-to-all-done.2) | copy-start | bytes 3932164
  119.4 48.3 %all-to-all-start.3 = ((bf16[16,3,64,256]{3,2,1,0:T(8,128)(2,1)}), bf16[16,3,64,256]{3,2,1,0:T(8,128)(2,1)S(1)}, u32[]{:S(2)}, u32[]{:S(2)}) async-start(bf16[16,3,64,256]{3,2,1,0:T(8,128)(2,1)} %shard_map.99), calls=%async_computation.3 | async-start | bytes 3145728 | tf_op jit(solution)/shard_map/all_to_all | solution.py:469
  129.2 62.5 %all-gather.4.cloned.1.call-start = ((), (), s32[]{:S(2)}) async-start(), calls=%async_computation.5 | async-start | bytes 2785280 | tf_op jit(solution)/shard_map/all_gather | solution.py:503
  187.5 21.6 %all-to-all-start.4 = ((bf16[16,64,256]{2,1,0:T(8,128)(2,1)}), bf16[16,64,256]{2,1,0:T(8,128)(2,1)S(1)}, u32[]{:S(2)}, u32[]{:S(2)}) async-start(bf16[16,64,256]{2,1,0:T(8,128)(2,1)} %shard_map.100), calls=%async_computation.4 | async-start | bytes 1048576 | tf_op jit(solution)/shard_map/all_to_all | solution.py:469
  (6 other events, 5.9 us)
Sparse Core Ops, SparseCore 0:
  48.0 64.0 all-gather.5
Sparse Core Ops, SparseCore 1:
  132.2 47.7 all-gather.3

commit v2 on v1

--- a/solution.py
+++ b/solution.py
@@ -97,11 +97,9 @@
         yield slice(16 * (n // 3), 16 * (n // 3) + 16), 128 * (n % 3), 16 * (n // 5), 128 * (n % 5)
 
 
-def cut_kernel(seq_ref, context_ref, qkv_ref, weights_ref, first_ref, last_ref, *refs):
-    *pieces, context, shard, last, done, sent = refs
+def pack_kernel(seq_ref, qkv_ref, weights_ref, packed_ref, shard, done, sent):
     core, chip = position(seq_ref)
-    chips = len(pieces) + 1
-    depth, half, width = weights_ref.shape[1], first_ref.shape[2], pieces[0].shape[1]
+    depth, half = weights_ref.shape[1], packed_ref.shape[2]
     inner = qkv_ref.shape[1] // 3
     shard[depth:, :] = jnp.zeros((shard.shape[0] - depth, half), jnp.bfloat16)
     loads = [
@@ -118,20 +116,51 @@
             pltpu.make_async_copy(
                 qkv_ref.at[pl.ds(first_row, 16), pl.ds(first_column, 128)],
                 shard.at[depth + low : depth + low + 16, left : left + 128],
-                done.at[3 + n],
+                done.at[1 + n],
             )
         )
-    load_context = pltpu.make_async_copy(context_ref, context, done.at[1])
-    load_last = pltpu.make_async_copy(weights_ref.at[1], last, done.at[2])
-    for load in (*loads, load_context, load_last):
+    for load in loads:
         load.start()
     for load in loads:
         load.wait()
     stores = []
-    for i in range(first_ref.shape[0]):
-        stores.append(pltpu.make_async_copy(shard, first_ref.at[i], sent.at[chips + i]))
+    for i in range(packed_ref.shape[0]):
+        stores.append(pltpu.make_async_copy(shard, packed_ref.at[i], sent.at[i]))
         stores[-1].start()
+    for store in stores:
+        store.wait()
+
+
+def pack(seq, qkv_weight, out_weights, steps):
+    _, depth, width = out_weights.shape
+    shape = (steps, depth + 32, width // 2)
+    far = pl.BlockSpec(memory_space=pl.ANY)
+    return pl.pallas_call(
+        pack_kernel,
+        out_shape=jax.ShapeDtypeStruct(shape, jnp.bfloat16),
+        in_specs=[pl.BlockSpec(memory_space=pltpu.SMEM)] + [far] * 2,
+        out_specs=far,
+        scratch_shapes=[
+            pltpu.VMEM(shape[1:], jnp.bfloat16),
+            pltpu.SemaphoreType.DMA((10,)),
+            pltpu.SemaphoreType.DMA((steps,)),
+        ],
+        compiler_params=pltpu.CompilerParams(vmem_limit_bytes=GRANT),
+        cost_estimate=pl.CostEstimate(flops=0, bytes_accessed=2 * 2**20, transcendentals=0),
+    )(seq, qkv_weight, out_weights)
+
+
+def cut_kernel(seq_ref, context_ref, weights_ref, last_ref, *refs):
+    *pieces, context, last, done, sent = refs
+    _, chip = position(seq_ref)
+    chips = len(pieces) + 1
+    width = pieces[0].shape[1]
+    load_context = pltpu.make_async_copy(context_ref, context, done.at[0])
+    load_last = pltpu.make_async_copy(weights_ref.at[1], last, done.at[1])
+    load_context.start()
+    load_last.start()
     load_context.wait()
+    stores = []
     for k, piece in enumerate(pieces):
         target = lax.rem(chip + k + 1, chips)
         tokens = pl.ds(pl.multiple_of(target * width, width), width)
@@ -144,26 +173,25 @@
         store.wait()
 
 
-def cut(seq, context, qkv_weight, out_weights, steps, chips):
+def cut(seq, context, out_weights, chips):
     dim, tokens = context.shape
     _, depth, width = out_weights.shape
     far = pl.BlockSpec(memory_space=pl.ANY)
-    shapes = [(steps, depth + 32, width // 2), (depth, width)] + [(dim, tokens // chips)] * (chips - 1)
+    shapes = [(depth, width)] + [(dim, tokens // chips)] * (chips - 1)
     return pl.pallas_call(
         cut_kernel,
         out_shape=[jax.ShapeDtypeStruct(shape, jnp.bfloat16) for shape in shapes],
-        in_specs=[pl.BlockSpec(memory_space=pltpu.SMEM)] + [far] * 3,
+        in_specs=[pl.BlockSpec(memory_space=pltpu.SMEM)] + [far] * 2,
         out_specs=[far] * len(shapes),
         scratch_shapes=[
             pltpu.VMEM(context.shape, jnp.bfloat16),
-            pltpu.VMEM(shapes[0][1:], jnp.bfloat16),
-            pltpu.VMEM(shapes[1], jnp.bfloat16),
-            pltpu.SemaphoreType.DMA((12,)),
-            pltpu.SemaphoreType.DMA((chips + steps,)),
+            pltpu.VMEM(shapes[0], jnp.bfloat16),
+            pltpu.SemaphoreType.DMA((2,)),
+            pltpu.SemaphoreType.DMA((chips,)),
         ],
         compiler_params=pltpu.CompilerParams(vmem_limit_bytes=GRANT),
-        cost_estimate=pl.CostEstimate(flops=0, bytes_accessed=4 * 2**20, transcendentals=0),
-    )(seq, context, qkv_weight, out_weights)
+        cost_estimate=pl.CostEstimate(flops=0, bytes_accessed=2 * 2**20, transcendentals=0),
+    )(seq, context, out_weights)
 
 
 def collect_kernel(seq_ref, context_ref, *refs):
@@ -480,10 +508,8 @@
     pairs = [(i, i ^ 1) for i in range(seqs)]
     heads_tokens = context[0].T
 
-    first_half, last_shard, *pieces = cut(
-        place, heads_tokens, qkv_weight, out_weights, steps, chips
-    )
-    packed = swap(first_half, "step")
+    packed = swap(pack(place, qkv_weight, out_weights, steps), "step")
+    last_shard, *pieces = cut(place, heads_tokens, out_weights, chips)
 
     pieces = [
         lax.ppermute(piece, "seq", [(i, (i + 2 * k + 2) % seqs) for i in range(seqs)])

time: 223 us -> 223 us (level)
  waiting for transfers between devices: 109 us -> 105 us
    all_to_all x5, waiting for transfers between devices: 93.7 us -> 90.4 us  [swap(): return lax.all_to_all(blocks, axis, split_axis=0, concat_axis=0, tiled=True)]
    pallas_call x0 -> x1, Pallas kernels: none -> 2.55 us  [pack(): pl.pallas_call(pack_kernel, out_shape=jax.ShapeDtypeStruct(shape, jnp.bfl...]
    all_to_all x5, starting transfers between devices: 29.3 us -> 31.6 us  [swap(): return lax.all_to_all(blocks, axis, split_axis=0, concat_axis=0, tiled=True)]
  transfers between devices with their start and end apart: 16 -> 16, of which waited for: 8 -> 7; matrix products, arithmetic and copies ran while one was open for 0% -> 0% of each run, Pallas kernels for 11% -> 12%
where the time goes in v2:
time: 223 us; the launch traced here: 222 us
  waiting for transfers between devices  105 us (47%)
  starting transfers between devices  51.6 us (23%)
  Pallas kernels  43.9 us (20%)
  between operations  15.7 us (7%)
  local copies, waits for them, and re-layouts  5.84 us (3%)
    all_to_all x5, waiting for transfers between devices, swap(): return lax.all_to_all(blocks, axis, split_axis=0, concat_axis=0, tiled=True)  90.4 us
    all_to_all x5, starting transfers between devices, swap(): return lax.all_to_all(blocks, axis, split_axis=0, concat_axis=0, tiled=True)  31.6 us
    pallas_call x1, Pallas kernels, attend(): pl.pallas_call(attention_kernel, out_shape=jax.ShapeDtypeStruct((blocks,...  19.8 us
    ppermute x7, starting transfers between devices, local(): lax.ppermute(piece, 'seq', [(i, (i + 2 * k + 2) % seqs) for i in range(se...  16.5 us
    pallas_call x1, Pallas kernels, project_qkv(): pl.pallas_call(qkv_kernel, out_shape=jax.ShapeDtypeStruct(shape, jnp.bflo...  7.3 us
    ppermute x7, waiting for transfers between devices, local(): lax.ppermute(piece, 'seq', [(i, (i + 2 * k + 2) % seqs) for i in range(se...  7.23 us
    unnamed x28, local copies, waits for them, and re-layouts  5.23 us
    pallas_call x1, Pallas kernels, mix(): pl.pallas_call(mix_kernel, out_shape=(jax.ShapeDtypeStruct(advanced.shape...  5.15 us
  transfers between devices with their start and end apart: 16, of which 7 were waited for; matrix products, arithmetic and copies ran while one was open for 0% of the time, Pallas kernels for 12%

profile of v2, /device:TPU:1, one launch (start us, length us, event | category | flops | bytes accessed | tf_op | source)
XLA Modules:
  0.0 222.3 jit_solution(4349189450369747012)
XLA Ops:
  8.0 2.6 %shard_map.96 = bf16[16,96,640]{2,1,0:T(8,128)(2,1)} custom-call(s32[1]{0:T(128)} %bitcast.seq_ref, bf16[80,3072]{1,0:T(8,128)(2,1)} %qkv_ref.1, bf16[2,64,1280]{2,1,0:T(8,128)(2,1)} %weights_ref.3), custom_call_target="tpu_custom_call" | custom-call | bytes 2097152 | tf_op jit(solution)/shard_map/pallas_call | solution.py:138
  10.6 7.6 %all-to-all-start = ((bf16[16,96,640]{2,1,0:T(8,128)(2,1)}), bf16[16,96,640]{2,1,0:T(8,128)(2,1)S(1)}, u32[]{:S(2)}, u32[]{:S(2)}) async-start(bf16[16,96,640]{2,1,0:T(8,128)(2,1)} %shard_map.96), calls=%async_computation | async-start | bytes 3932160 | tf_op jit(solution)/shard_map/all_to_all | solution.py:497
  18.2 1.9 shard_map.95
  21.9 3.0 %collective-permute-start.1 = (bf16[64,512]{1,0:T(8,128)(2,1)}, bf16[64,512]{1,0:T(8,128)(2,1)S(1)}, u32[]{:S(2)}, u32[]{:S(2)}) collective-permute-start(bf16[64,512]{1,0:T(8,128)(2,1)} %get-tuple-element.17), channel_id=1, source_target_pairs={{0,4},{1,5},{2,6},{3,7},{4,8},{5,9},{6,10},{7,11},{8,12},{9,13},{1... | collective-permute-start | bytes 196616 | tf_op jit(solution)/shard_map/ppermute | solution.py:515
  24.9 3.8 %collective-permute-start.2 = (bf16[64,512]{1,0:T(8,128)(2,1)}, bf16[64,512]{1,0:T(8,128)(2,1)S(1)}, u32[]{:S(2)}, u32[]{:S(2)}) collective-permute-start(bf16[64,512]{1,0:T(8,128)(2,1)} %get-tuple-element.18), channel_id=1, source_target_pairs={{0,6},{1,7},{2,8},{3,9},{4,10},{5,11},{6,12},{7,13},{8,14},{9,15},... | collective-permute-start | bytes 196616 | tf_op jit(solution)/shard_map/ppermute | solution.py:515
  29.1 4.5 %collective-permute-start.4 = (bf16[64,512]{1,0:T(8,128)(2,1)}, bf16[64,512]{1,0:T(8,128)(2,1)S(1)}, u32[]{:S(2)}, u32[]{:S(2)}) collective-permute-start(bf16[64,512]{1,0:T(8,128)(2,1)} %get-tuple-element.20), channel_id=1, source_target_pairs={{0,10},{1,11},{2,12},{3,13},{4,14},{5,15},{6,0},{7,1},{8,2},{9,3},... | collective-permute-start | bytes 196616 | tf_op jit(solution)/shard_map/ppermute | solution.py:515
  33.6 2.4 %collective-permute-start.5 = (bf16[64,512]{1,0:T(8,128)(2,1)}, bf16[64,512]{1,0:T(8,128)(2,1)S(1)}, u32[]{:S(2)}, u32[]{:S(2)}) collective-permute-start(bf16[64,512]{1,0:T(8,128)(2,1)} %get-tuple-element.21), channel_id=1, source_target_pairs={{0,12},{1,13},{2,14},{3,15},{4,0},{5,1},{6,2},{7,3},{8,4},{9,5},{1... | collective-permute-start | bytes 196616 | tf_op jit(solution)/shard_map/ppermute | solution.py:515
  36.7 7.2 %collective-permute-done.5.refs_5_ = bf16[64,512]{1,0:T(8,128)(2,1)S(1)} collective-permute-done((bf16[64,512]{1,0:T(8,128)(2,1)}, bf16[64,512]{1,0:T(8,128)(2,1)S(1)}, u32[]{:S(2)}, u32[]{:S(2)}) %collective-permute-start.5) | collective-permute-done | bytes 65568 | tf_op jit(solution)/shard_map/ppermute | solution.py:515
  45.9 2.3 %shard_map.97 = (bf16[8,64,256]{2,1,0:T(8,128)(2,1)}, bf16[8,64,256]{2,1,0:T(8,128)(2,1)}, bf16[16,48,384]{2,1,0:T(8,128)(2,1)}, bf16[16,96,640]{2,1,0:T(8,128)(2,1)}) custom-call(s32[1]{0:T(128)} %bitcast.seq_ref, bf16[64,4096]{1,0:T(8,128)(2,1)} %bitcast.18, bf16[64,512]{1,0:T(8,128)(2,1)} %copy-done.7, ...), custom_call_target="tpu_custom_call", output_to_operand_aliasing={{3}: (9, {})} | custom-call | bytes 1048576 | tf_op jit(solution)/shard_map/pallas_call | solution.py:239
  48.2 3.3 %collective-permute-start.8 = (bf16[16,96,640]{2,1,0:T(8,128)(2,1)}, bf16[16,96,640]{2,1,0:T(8,128)(2,1)S(1)}, u32[]{:S(2)}, u32[]{:S(2)}) collective-permute-start(bf16[16,96,640]{2,1,0:T(8,128)(2,1)} %get-tuple-element.25.mine_ref), channel_id=1, source_target_pairs={{0,1},{1,0},{2,3},{3,2},{4,5},{5,4},{6,7},{7,6},{8,9},{9,8},{10,11... | collective-permute-start | bytes 5898248 | tf_op jit(solution)/shard_map/ppermute | solution.py:521
  51.6 4.1 %collective-permute-done.7.taken_ref = bf16[8,64,256]{2,1,0:T(8,128)(2,1)S(1)} collective-permute-done((bf16[8,64,256]{2,1,0:T(8,128)(2,1)}, bf16[8,64,256]{2,1,0:T(8,128)(2,1)S(1)}, u32[]{:S(2)}, u32[]{:S(2)}) %collective-permute-start.7) | collective-permute-done | bytes 262176 | tf_op jit(solution)/shard_map/ppermute | solution.py:520
  57.2 4.8 %shard_map.98 = f32[256,1280]{1,0:T(8,128)} custom-call(s32[1]{0:T(128)} %bitcast.seq_ref, f32[3]{0:T(128)} %bitcast.22, bf16[8,64,256]{2,1,0:T(8,128)(2,1)} %get-tuple-element.23.kept_ref, bf16[8,64,256]{2,1,0:T(8,128)(2,1)} %copy-done.6, bf16[16,96,640]{2,1,0:T(8,128)(2,1)} %get-tuple-element.25.mine_ref, bf16[16,96,640]{2,1,0:T(8,128)(2,1)} %copy-done.5, ...), custom_call_target="tpu_custom_call" | custom-call | flops 671088640 | bytes 8388608 | tf_op jit(solution)/shard_map/pallas_call | solution.py:306
  61.9 4.7 %all-to-all-start.1 = ((f32[16,16,1280]{2,1,0:T(8,128)}), f32[16,16,1280]{2,1,0:T(8,128)S(1)}, u32[]{:S(2)}, u32[]{:S(2)}) async-start(f32[16,16,1280]{2,1,0:T(8,128)} %bitcast.16), calls=%async_computation.1 | async-start | bytes 2621440 | tf_op jit(solution)/shard_map/all_to_all | solution.py:497
  66.7 18.2 %all-to-all-done.1.drifts_ref = f32[16,16,1280]{2,1,0:T(8,128)S(1)} async-done(((f32[16,16,1280]{2,1,0:T(8,128)}), f32[16,16,1280]{2,1,0:T(8,128)S(1)}, u32[]{:S(2)}, u32[]{:S(2)}) %all-to-all-start.1) | async-done | bytes 1310752 | tf_op jit(solution)/shard_map/all_to_all | solution.py:497
  86.1 5.1 %all-to-all-start.2 = ((f32[16,16,1280]{2,1,0:T(8,128)}), f32[16,16,1280]{2,1,0:T(8,128)S(1)}, u32[]{:S(2)}, u32[]{:S(2)}) async-start(f32[16,16,1280]{2,1,0:T(8,128)} %copy-done.1), calls=%async_computation.2 | async-start | bytes 2621440 | tf_op jit(solution)/shard_map/all_to_all | solution.py:497
  91.8 17.0 %all-to-all-done.2 = f32[16,16,1280]{2,1,0:T(8,128)S(1)} async-done(((f32[16,16,1280]{2,1,0:T(8,128)}), f32[16,16,1280]{2,1,0:T(8,128)S(1)}, u32[]{:S(2)}, u32[]{:S(2)}) %all-to-all-start.2) | async-done | bytes 1310752 | tf_op jit(solution)/shard_map/all_to_all | solution.py:497
  108.8 3.0 %all-gather.6.cloned.1.call-done = bf16[256,48,384]{2,1,0:T(8,128)(2,1)} async-done(((bf16[16,48,384]{2,1,0:T(8,128)(2,1)}), bf16[256,48,384]{2,1,0:T(8,128)(2,1)}) %all-gather.6.cloned.1.call-update) | async-done | bytes 9437200 | tf_op jit(solution)/shard_map/all_gather | solution.py:519
  111.8 7.3 %shard_map.100 = bf16[16,3,64,256]{3,2,1,0:T(8,128)(2,1)} custom-call(f32[256,1280]{1,0:T(8,128)} %bitcast.13, f32[1,1280]{1,0:T(1,128)} %reshape.22.gain_ref, bf16[16,16,48,384]{3,2,1,0:T(8,128)(2,1)} %bitcast.15), custom_call_target="tpu_custom_call" | custom-call | flops 2013265920 | bytes 10485760 | tf_op jit(solution)/shard_map/pallas_call | solution.py:417
  119.1 9.9 %all-to-all-start.3 = ((bf16[16,3,64,256]{3,2,1,0:T(8,128)(2,1)}), bf16[16,3,64,256]{3,2,1,0:T(8,128)(2,1)S(1)}, u32[]{:S(2)}, u32[]{:S(2)}) async-start(bf16[16,3,64,256]{3,2,1,0:T(8,128)(2,1)} %shard_map.100), calls=%async_computation.3 | async-start | bytes 3145728 | tf_op jit(solution)/shard_map/all_to_all | solution.py:497
  129.6 37.9 %all-to-all-done.3.qkv_ref = bf16[16,3,64,256]{3,2,1,0:T(8,128)(2,1)S(1)} async-done(((bf16[16,3,64,256]{3,2,1,0:T(8,128)(2,1)}), bf16[16,3,64,256]{3,2,1,0:T(8,128)(2,1)S(1)}, u32[]{:S(2)}, u32[]{:S(2)}) %all-to-all-start.3) | async-done | bytes 1572896 | tf_op jit(solution)/shard_map/all_to_all | solution.py:497
  167.5 19.8 %shard_map.101 = bf16[16,64,256]{2,1,0:T(8,128)(2,1)} custom-call(bf16[16,3,64,256]{3,2,1,0:T(8,128)(2,1)S(1)} %all-to-all-done.3.qkv_ref), custom_call_target="tpu_custom_call" | custom-call | flops 17179869184 | bytes 3145728 | tf_op jit(solution)/shard_map/pallas_call | solution.py:71
  187.3 4.3 %all-to-all-start.4 = ((bf16[16,64,256]{2,1,0:T(8,128)(2,1)}), bf16[16,64,256]{2,1,0:T(8,128)(2,1)S(1)}, u32[]{:S(2)}, u32[]{:S(2)}) async-start(bf16[16,64,256]{2,1,0:T(8,128)(2,1)} %shard_map.101), calls=%async_computation.4 | async-start | bytes 1048576 | tf_op jit(solution)/shard_map/all_to_all | solution.py:497
  191.6 17.3 %all-to-all-done.4 = bf16[16,64,256]{2,1,0:T(8,128)(2,1)S(1)} async-done(((bf16[16,64,256]{2,1,0:T(8,128)(2,1)}), bf16[16,64,256]{2,1,0:T(8,128)(2,1)S(1)}, u32[]{:S(2)}, u32[]{:S(2)}) %all-to-all-start.4) | async-done | bytes 524320 | tf_op jit(solution)/shard_map/all_to_all | solution.py:497
  209.6 5.2 %shard_map.102 = (f32[256,1280]{1,0:T(8,128)}, f32[256,1280]{1,0:T(8,128)}) custom-call(bf16[1024,256]{1,0:T(8,128)(2,1)} %bitcast.19, bf16[1024,1280]{1,0:T(8,128)(2,1)} %all-gather.4.cloned.1.call-done.weight_ref, f32[256,1280]{1,0:T(8,128)} %bitcast.14), custom_call_target="tpu_custom_call" | custom-call | flops 671088640 | bytes 8388608 | tf_op jit(solution)/shard_map/pallas_call | solution.py:477
  (48 shorter events, 9.6 us)
Async XLA Ops:
  8.0 58.7 %copy-start = (f32[256,1280]{1,0:T(8,128)S(1)}, f32[256,1280]{1,0:T(8,128)}, u32[]{:S(2)}) copy-start(f32[256,1280]{1,0:T(8,128)} %param.9) | copy-start | bytes 3932164
  10.6 34.0 %all-to-all-start = ((bf16[16,96,640]{2,1,0:T(8,128)(2,1)}), bf16[16,96,640]{2,1,0:T(8,128)(2,1)S(1)}, u32[]{:S(2)}, u32[]{:S(2)}) async-start(bf16[16,96,640]{2,1,0:T(8,128)(2,1)} %shard_map.96), calls=%async_computation | async-start | bytes 3932160 | tf_op jit(solution)/shard_map/all_to_all | solution.py:497
  18.2 93.6 %all-gather.6.cloned.1.call-start = ((), (), s32[]{:S(2)}) async-start(), calls=%async_computation.6 | async-start | bytes 10027008 | tf_op jit(solution)/shard_map/all_gather | solution.py:519
  20.2 13.4 %collective-permute-start = (bf16[64,512]{1,0:T(8,128)(2,1)}, bf16[64,512]{1,0:T(8,128)(2,1)S(1)}, u32[]{:S(2)}, u32[]{:S(2)}) collective-permute-start(bf16[64,512]{1,0:T(8,128)(2,1)} %get-tuple-element.16), channel_id=1, source_target_pairs={{0,2},{1,3},{2,4},{3,5},{4,6},{5,7},{6,8},{7,9},{8,10},{9,11},{10,... | collective-permute-start | bytes 196616 | tf_op jit(solution)/shard_map/ppermute | solution.py:515
  21.9 14.1 %collective-permute-start.1 = (bf16[64,512]{1,0:T(8,128)(2,1)}, bf16[64,512]{1,0:T(8,128)(2,1)S(1)}, u32[]{:S(2)}, u32[]{:S(2)}) collective-permute-start(bf16[64,512]{1,0:T(8,128)(2,1)} %get-tuple-element.17), channel_id=1, source_target_pairs={{0,4},{1,5},{2,6},{3,7},{4,8},{5,9},{6,10},{7,11},{8,12},{9,13},{1... | collective-permute-start | bytes 196616 | tf_op jit(solution)/shard_map/ppermute | solution.py:515
  24.9 11.8 %collective-permute-start.2 = (bf16[64,512]{1,0:T(8,128)(2,1)}, bf16[64,512]{1,0:T(8,128)(2,1)S(1)}, u32[]{:S(2)}, u32[]{:S(2)}) collective-permute-start(bf16[64,512]{1,0:T(8,128)(2,1)} %get-tuple-element.18), channel_id=1, source_target_pairs={{0,6},{1,7},{2,8},{3,9},{4,10},{5,11},{6,12},{7,13},{8,14},{9,15},... | collective-permute-start | bytes 196616 | tf_op jit(solution)/shard_map/ppermute | solution.py:515
  28.6 8.1 %collective-permute-start.3 = (bf16[64,512]{1,0:T(8,128)(2,1)}, bf16[64,512]{1,0:T(8,128)(2,1)S(1)}, u32[]{:S(2)}, u32[]{:S(2)}) collective-permute-start(bf16[64,512]{1,0:T(8,128)(2,1)} %get-tuple-element.19), channel_id=1, source_target_pairs={{0,8},{1,9},{2,10},{3,11},{4,12},{5,13},{6,14},{7,15},{8,0},{9,1},... | collective-permute-start | bytes 196616 | tf_op jit(solution)/shard_map/ppermute | solution.py:515
  29.1 7.6 %collective-permute-start.4 = (bf16[64,512]{1,0:T(8,128)(2,1)}, bf16[64,512]{1,0:T(8,128)(2,1)S(1)}, u32[]{:S(2)}, u32[]{:S(2)}) collective-permute-start(bf16[64,512]{1,0:T(8,128)(2,1)} %get-tuple-element.20), channel_id=1, source_target_pairs={{0,10},{1,11},{2,12},{3,13},{4,14},{5,15},{6,0},{7,1},{8,2},{9,3},... | collective-permute-start | bytes 196616 | tf_op jit(solution)/shard_map/ppermute | solution.py:515
  33.6 11.0 %copy-start.7 = (bf16[64,512]{1,0:T(8,128)(2,1)}, bf16[64,512]{1,0:T(8,128)(2,1)S(1)}, u32[]{:S(2)}) copy-start(bf16[64,512]{1,0:T(8,128)(2,1)S(1)} %collective-permute-done.refs_0_) | copy-start | bytes 196612
  33.6 10.4 %collective-permute-start.5 = (bf16[64,512]{1,0:T(8,128)(2,1)}, bf16[64,512]{1,0:T(8,128)(2,1)S(1)}, u32[]{:S(2)}, u32[]{:S(2)}) collective-permute-start(bf16[64,512]{1,0:T(8,128)(2,1)} %get-tuple-element.21), channel_id=1, source_target_pairs={{0,12},{1,13},{2,14},{3,15},{4,0},{5,1},{6,2},{7,3},{8,4},{9,5},{1... | collective-permute-start | bytes 196616 | tf_op jit(solution)/shard_map/ppermute | solution.py:515
  36.0 8.6 %copy-start.8 = (bf16[64,512]{1,0:T(8,128)(2,1)}, bf16[64,512]{1,0:T(8,128)(2,1)S(1)}, u32[]{:S(2)}) copy-start(bf16[64,512]{1,0:T(8,128)(2,1)S(1)} %collective-permute-done.1.refs_1_) | copy-start | bytes 196612
  36.0 8.6 %collective-permute-start.6 = (bf16[64,512]{1,0:T(8,128)(2,1)}, bf16[64,512]{1,0:T(8,128)(2,1)}, u32[]{:S(2)}, u32[]{:S(2)}) collective-permute-start(bf16[64,512]{1,0:T(8,128)(2,1)} %get-tuple-element.22), channel_id=1, source_target_pairs={{0,14},{1,15},{2,0},{3,1},{4,2},{5,3},{6,4},{7,5},{8,6},{9,7},{10,... | collective-permute-start | bytes 196616 | tf_op jit(solution)/shard_map/ppermute | solution.py:515
  36.7 7.9 %copy-start.9 = (bf16[64,512]{1,0:T(8,128)(2,1)}, bf16[64,512]{1,0:T(8,128)(2,1)S(1)}, u32[]{:S(2)}) copy-start(bf16[64,512]{1,0:T(8,128)(2,1)S(1)} %collective-permute-done.2.refs_2_) | copy-start | bytes 196612
  36.7 7.9 %copy-start.10 = (bf16[64,512]{1,0:T(8,128)(2,1)}, bf16[64,512]{1,0:T(8,128)(2,1)S(1)}, u32[]{:S(2)}) copy-start(bf16[64,512]{1,0:T(8,128)(2,1)S(1)} %collective-permute-done.3.refs_3_) | copy-start | bytes 196612
  36.7 7.2 %copy-start.11 = (bf16[64,512]{1,0:T(8,128)(2,1)}, bf16[64,512]{1,0:T(8,128)(2,1)S(1)}, u32[]{:S(2)}) copy-start(bf16[64,512]{1,0:T(8,128)(2,1)S(1)} %collective-permute-done.4.refs_4_) | copy-start | bytes 196612
  48.2 7.5 %collective-permute-start.8 = (bf16[16,96,640]{2,1,0:T(8,128)(2,1)}, bf16[16,96,640]{2,1,0:T(8,128)(2,1)S(1)}, u32[]{:S(2)}, u32[]{:S(2)}) collective-permute-start(bf16[16,96,640]{2,1,0:T(8,128)(2,1)} %get-tuple-element.25.mine_ref), channel_id=1, source_target_pairs={{0,1},{1,0},{2,3},{3,2},{4,5},{5,4},{6,7},{7,6},{8,9},{9,8},{10,11... | collective-permute-start | bytes 5898248 | tf_op jit(solution)/shard_map/ppermute | solution.py:521
  51.5 4.2 %collective-permute-start.7 = (bf16[8,64,256]{2,1,0:T(8,128)(2,1)}, bf16[8,64,256]{2,1,0:T(8,128)(2,1)S(1)}, u32[]{:S(2)}, u32[]{:S(2)}) collective-permute-start(bf16[8,64,256]{2,1,0:T(8,128)(2,1)} %get-tuple-element.24), channel_id=1, source_target_pairs={{0,1},{1,0},{2,3},{3,2},{4,5},{5,4},{6,7},{7,6},{8,9},{9,8},{10,11... | collective-permute-start | bytes 786440 | tf_op jit(solution)/shard_map/ppermute | solution.py:520
  61.9 23.0 %all-to-all-start.1 = ((f32[16,16,1280]{2,1,0:T(8,128)}), f32[16,16,1280]{2,1,0:T(8,128)S(1)}, u32[]{:S(2)}, u32[]{:S(2)}) async-start(f32[16,16,1280]{2,1,0:T(8,128)} %bitcast.16), calls=%async_computation.1 | async-start | bytes 2621440 | tf_op jit(solution)/shard_map/all_to_all | solution.py:497
  86.1 5.1 %copy-start.13 = (f32[1280]{0:T(1024)S(1)}, f32[1280]{0:T(1024)}, u32[]{:S(2)}) copy-start(f32[1280]{0:T(1024)} %param.15) | copy-start | bytes 15364
  86.1 22.7 %all-to-all-start.2 = ((f32[16,16,1280]{2,1,0:T(8,128)}), f32[16,16,1280]{2,1,0:T(8,128)S(1)}, u32[]{:S(2)}, u32[]{:S(2)}) async-start(f32[16,16,1280]{2,1,0:T(8,128)} %copy-done.1), calls=%async_computation.2 | async-start | bytes 2621440 | tf_op jit(solution)/shard_map/all_to_all | solution.py:497
  108.8 3.0 %copy-start.3 = (f32[16,16,1280]{2,1,0:T(8,128)}, f32[16,16,1280]{2,1,0:T(8,128)S(1)}, u32[]{:S(2)}) copy-start(f32[16,16,1280]{2,1,0:T(8,128)S(1)} %all-to-all-done.2) | copy-start | bytes 3932164
  119.1 48.3 %all-to-all-start.3 = ((bf16[16,3,64,256]{3,2,1,0:T(8,128)(2,1)}), bf16[16,3,64,256]{3,2,1,0:T(8,128)(2,1)S(1)}, u32[]{:S(2)}, u32[]{:S(2)}) async-start(bf16[16,3,64,256]{3,2,1,0:T(8,128)(2,1)} %shard_map.100), calls=%async_computation.3 | async-start | bytes 3145728 | tf_op jit(solution)/shard_map/all_to_all | solution.py:497
  129.0 62.5 %all-gather.4.cloned.1.call-start = ((), (), s32[]{:S(2)}) async-start(), calls=%async_computation.5 | async-start | bytes 2785280 | tf_op jit(solution)/shard_map/all_gather | solution.py:529
  187.3 21.6 %all-to-all-start.4 = ((bf16[16,64,256]{2,1,0:T(8,128)(2,1)}), bf16[16,64,256]{2,1,0:T(8,128)(2,1)S(1)}, u32[]{:S(2)}, u32[]{:S(2)}) async-start(bf16[16,64,256]{2,1,0:T(8,128)(2,1)} %shard_map.101), calls=%async_computation.4 | async-start | bytes 1048576 | tf_op jit(solution)/shard_map/all_to_all | solution.py:497
  (6 other events, 5.9 us)
Sparse Core Ops, SparseCore 0:
  48.3 63.4 all-gather.5
Sparse Core Ops, SparseCore 1:
  132.0 47.7 all-gather.3
